TPU v7x, 32 devices: a whole 2x2x4 slice. The times are simulated.
32 devices in a mesh: seq: 2 (over x), dp: 16 (over z, y, core).
Axes of the slice: x: 2, y: 2, z: 4, core: 2. Of those that a mesh axis runs over, the one named last changes fastest.
Arguments:
- characters: bfloat16 [2, 16, 1024, 768], P(None, 'dp', 'seq'), may hold values from -6 to 6
- pre_gain: bfloat16 [768], P(('seq', 'dp')), may hold values from 0.5 to 1.5
- pre_shift: bfloat16 [768], P(('seq', 'dp')), may hold values from -3 to 3
- w_query: bfloat16 [768, 768], P(('seq', 'dp')), may hold values from -0.3125 to 0.3125
- b_query: bfloat16 [768], P(('seq', 'dp')), may hold values from -3 to 3
- w_key: bfloat16 [768, 768], P(('seq', 'dp')), may hold values from -0.3125 to 0.3125
- w_value: bfloat16 [768, 768], P(('seq', 'dp')), may hold values from -0.21875 to 0.21875
- b_value: bfloat16 [768], P(('seq', 'dp')), may hold values from -3 to 3
- w_output: bfloat16 [768, 768], P(('seq', 'dp')), may hold values from -0.625 to 0.625
- b_output: bfloat16 [768], P(('seq', 'dp')), may hold values from -3 to 3
- mid_gain: bfloat16 [768], P(('seq', 'dp')), may hold values from 0.5 to 1.5
- mid_shift: bfloat16 [768], P(('seq', 'dp')), may hold values from -3 to 3
- w_up: bfloat16 [768, 3072], P(('seq', 'dp')), may hold values from -0.21875 to 0.21875
- b_up: bfloat16 [3072], P(('seq', 'dp')), may hold values from -3 to 3
- w_down: bfloat16 [3072, 768], P(('seq', 'dp')), may hold values from -0.109375 to 0.109375
- b_down: bfloat16 [768], P(('seq', 'dp')), may hold values from -3 to 3
- w_conv: bfloat16 [3072, 768], P(('seq', 'dp')), may hold values from -0.109375 to 0.109375
- b_conv: bfloat16 [768], P(('seq', 'dp')), may hold values from -3 to 3
- out_gain: bfloat16 [768], P(('seq', 'dp')), may hold values from 0.5 to 1.5
- out_shift: bfloat16 [768], P(('seq', 'dp')), may hold values from -3 to 3
- row_lengths: int32 [16, 4], P('dp'), may hold values from 0 to 1024, as said below
- row_batch: int32 [16, 4], P('dp'), may hold values from 0 to 1
- cot_molecules: bfloat16 [2, 16, 256, 768], P(None, 'dp', 'seq'), may hold values from -6 to 6
Outputs:
- molecules: bfloat16 [2, 16, 256, 768], P(None, 'dp', 'seq')
- grad_chars: float32 [2, 16, 1024, 768], P(None, 'dp', 'seq')
- grad_pre_gain: float32 [768], P(('seq', 'dp'))
- grad_pre_shift: float32 [768], P(('seq', 'dp'))
- grad_w_query: float32 [768, 768], P(('seq', 'dp'))
- grad_b_query: float32 [768], P(('seq', 'dp'))
- grad_w_key: float32 [768, 768], P(('seq', 'dp'))
- grad_w_value: float32 [768, 768], P(('seq', 'dp'))
- grad_b_value: float32 [768], P(('seq', 'dp'))
- grad_w_output: float32 [768, 768], P(('seq', 'dp'))
- grad_b_output: float32 [768], P(('seq', 'dp'))
- grad_mid_gain: float32 [768], P(('seq', 'dp'))
- grad_mid_shift: float32 [768], P(('seq', 'dp'))
- grad_w_up: float32 [768, 3072], P(('seq', 'dp'))
- grad_b_up: float32 [3072], P(('seq', 'dp'))
- grad_w_down: float32 [3072, 768], P(('seq', 'dp'))
- grad_b_down: float32 [768], P(('seq', 'dp'))
- grad_w_conv: float32 [3072, 768], P(('seq', 'dp'))
- grad_b_conv: float32 [768], P(('seq', 'dp'))
- grad_out_gain: float32 [768], P(('seq', 'dp'))
- grad_out_shift: float32 [768], P(('seq', 'dp'))
Inputs may be any that keep to these rules, and one draw needn't show every extreme that they name: `row_lengths`: each entry is 0, 512 or 1024; the rows of one group in one micro-batch add up to at most 1024; every group has a row of 1024.
All inputs are finite; a program needn't handle non-finite values.
Results may differ from a plain program's by a relative error of at most 0.018.
Values may be sent and summed in bfloat16 or wider, within the bound.
A program may use at most 256 MiB of HBM per device.

v0:
```python
import jax
import jax.numpy as jnp
from jax import lax
from jax.sharding import PartitionSpec as P

D = 768
HEADS = 12
HEAD = 64
KER = 4
WIN = 128


EPSILON = 1e-05


def with_halo(x, sides, width):
    for axis, dim in sides:
        size, length = (lax.axis_size(axis), x.shape[dim])
        up = [(i, (i + 1) % size) for i in range(size - 1)]
        down = [(j, i) for i, j in up]
        last = lax.slice_in_dim(x, length - width, length, axis=dim)
        initial = lax.slice_in_dim(x, 0, width, axis=dim)
        before = lax.ppermute(last, axis, up)
        after = lax.ppermute(initial, axis, down)
        x = jnp.concatenate([before, x, after], axis=dim)
    return x


def shifted(value, axis, steps):
    count = lax.axis_size(axis)
    initial, last = (max(0, -steps), min(count, count - steps))
    return lax.ppermute(value, axis, [(source, source + steps) for source in range(initial, last)])


def normalize(vector, gain, shift):
    average = jnp.mean(vector, axis=-1, keepdims=True)
    centered = vector - average
    variance = jnp.mean(centered * centered, axis=-1, keepdims=True)
    return centered * lax.rsqrt(variance + EPSILON) * gain + shift


def segment_ids(lengths, batches, micro_step, places):
    slot_ids = jnp.arange(lengths.shape[0], dtype=jnp.int32)
    before = (slot_ids[:, None] < slot_ids[None, :]) & (batches[:, None] == batches[None, :])
    starts = jnp.sum(jnp.where(before, lengths[:, None], 0), axis=0)
    inside = (
        (batches[:, None] == micro_step)
        & (places[None, :] >= starts[:, None])
        & (places[None, :] < (starts + lengths)[:, None])
    )
    return jnp.sum(jnp.where(inside, slot_ids[:, None] + 1, 0), axis=0) - 1


def forward_dot(left, right):
    return jnp.dot(left, right, preferred_element_type=jnp.float32)


def weight_grad(left, right):
    return lax.dot_general(
        left, right, (((0,), (0,)), ((), ())), preferred_element_type=jnp.float32
    )


def input_grad(left, weight):
    return lax.dot_general(
        left, weight, (((1,), (1,)), ((), ())), preferred_element_type=jnp.float32
    )


def band_rows(rows_all, block_count):
    return jnp.stack([rows_all[b * WIN : b * WIN + 3 * WIN] for b in range(block_count)])


def band_back(band_grads, block_count):
    total = None
    for b in range(block_count):
        padded = jnp.pad(band_grads[b], ((b * WIN, (block_count - 1 - b) * WIN), (0, 0), (0, 0)))
        total = padded if total is None else total + padded
    return total


def forward(weights_all, char_block, allowed):
    (
        pre_gain,
        pre_shift,
        w_query,
        b_query,
        w_key,
        w_value,
        b_value,
        w_output,
        b_output,
        mid_gain,
        mid_shift,
        w_up,
        b_up,
        w_down,
        b_down,
        w_conv,
        b_conv,
        out_gain,
        out_shift,
    ) = weights_all
    block_len = char_block.shape[0]
    block_count = block_len // WIN
    source = char_block.astype(jnp.float32)
    normed = normalize(source, pre_gain.astype(jnp.float32), pre_shift.astype(jnp.float32)).astype(
        jnp.bfloat16
    )
    queries = (forward_dot(normed, w_query) + b_query.astype(jnp.float32)).astype(jnp.bfloat16)
    key_rows = forward_dot(normed, w_key).astype(jnp.bfloat16)
    value_rows = (forward_dot(normed, w_value) + b_value.astype(jnp.float32)).astype(jnp.bfloat16)
    stacked = with_halo(jnp.stack([key_rows, value_rows]), (("seq", 1),), WIN)
    key_all = stacked[0].reshape(-1, HEADS, HEAD)
    value_all = stacked[1].reshape(-1, HEADS, HEAD)
    query_heads = queries.reshape(block_count, WIN, HEADS, HEAD)
    key_band = band_rows(key_all, block_count)
    value_band = band_rows(value_all, block_count)
    scores = jnp.einsum(
        "bqhe,bkhe->bhqk", query_heads, key_band, preferred_element_type=jnp.float32
    ) * HEAD ** (-0.5)
    scores = jnp.where(allowed[:, None], scores, -1e30)
    largest = jnp.max(scores, axis=-1, keepdims=True)
    powers = jnp.exp(scores - largest)
    norm_sum = jnp.sum(powers, axis=-1, keepdims=True)
    attend = powers / norm_sum
    logsum = largest + jnp.log(norm_sum)
    mixture = (
        jnp.einsum(
            "bhqk,bkhe->bqhe",
            attend.astype(jnp.bfloat16),
            value_band,
            preferred_element_type=jnp.float32,
        )
        .reshape(block_len, D)
        .astype(jnp.bfloat16)
    )
    residual = source + (forward_dot(mixture, w_output) + b_output.astype(jnp.float32))
    normed2 = normalize(
        residual, mid_gain.astype(jnp.float32), mid_shift.astype(jnp.float32)
    ).astype(jnp.bfloat16)
    hidden = forward_dot(normed2, w_up) + b_up.astype(jnp.float32)
    active = jax.nn.gelu(hidden).astype(jnp.bfloat16)
    residual2 = residual + (forward_dot(active, w_down) + b_down.astype(jnp.float32))
    grouped = residual2.astype(jnp.bfloat16).reshape(block_len // KER, KER * D)
    conv_out = forward_dot(grouped, w_conv) + b_conv.astype(jnp.float32)
    curved = jax.nn.gelu(conv_out)
    result = normalize(curved, out_gain.astype(jnp.float32), out_shift.astype(jnp.float32))
    kept = (
        source,
        normed,
        query_heads,
        key_all,
        value_all,
        logsum,
        mixture,
        residual,
        normed2,
        hidden,
        active,
        grouped,
        conv_out,
        curved,
    )
    return (result.astype(jnp.bfloat16), kept)


def backward(weights_back, kept, cot_block, allowed):
    (
        pre_gain,
        pre_shift,
        w_query,
        b_query,
        w_key,
        w_value,
        b_value,
        w_output,
        b_output,
        mid_gain,
        mid_shift,
        w_up,
        b_up,
        w_down,
        b_down,
        w_conv,
        b_conv,
        out_gain,
        out_shift,
    ) = weights_back
    (
        source,
        normed,
        query_heads,
        key_all,
        value_all,
        logsum,
        mixture,
        residual,
        normed2,
        hidden,
        active,
        grouped,
        conv_out,
        curved,
    ) = kept
    block_len = source.shape[0]
    block_count = block_len // WIN
    _, pullback = jax.vjp(
        normalize, curved, out_gain.astype(jnp.float32), out_shift.astype(jnp.float32)
    )
    d_curved, g_out_gain, g_out_shift = pullback(cot_block.astype(jnp.float32))
    _, pullback = jax.vjp(jax.nn.gelu, conv_out)
    (d_conv,) = pullback(d_curved)
    g_b_conv = jnp.sum(d_conv, axis=0)
    d_conv_low = d_conv.astype(jnp.bfloat16)
    g_w_conv = weight_grad(grouped, d_conv_low)
    d_res2 = input_grad(d_conv_low, w_conv).reshape(block_len, D)
    g_b_down = jnp.sum(d_res2, axis=0)
    d_res2_low = d_res2.astype(jnp.bfloat16)
    g_w_down = weight_grad(active, d_res2_low)
    d_active = input_grad(d_res2_low, w_down)
    _, pullback = jax.vjp(jax.nn.gelu, hidden)
    (d_hidden,) = pullback(d_active)
    g_b_up = jnp.sum(d_hidden, axis=0)
    d_hidden_low = d_hidden.astype(jnp.bfloat16)
    g_w_up = weight_grad(normed2, d_hidden_low)
    d_normed2 = input_grad(d_hidden_low, w_up)
    _, pullback = jax.vjp(
        normalize, residual, mid_gain.astype(jnp.float32), mid_shift.astype(jnp.float32)
    )
    d_middle, g_mid_gain, g_mid_shift = pullback(d_normed2)
    d_res = d_res2 + d_middle
    g_b_output = jnp.sum(d_res, axis=0)
    d_res_low = d_res.astype(jnp.bfloat16)
    g_w_output = weight_grad(mixture, d_res_low)
    d_mix = (
        input_grad(d_res_low, w_output).astype(jnp.bfloat16).reshape(block_count, WIN, HEADS, HEAD)
    )
    key_band = band_rows(key_all, block_count)
    value_band = band_rows(value_all, block_count)
    scores = jnp.einsum(
        "bqhe,bkhe->bhqk", query_heads, key_band, preferred_element_type=jnp.float32
    ) * HEAD ** (-0.5)
    scores = jnp.where(allowed[:, None], scores, -1e30)
    attend = jnp.exp(scores - logsum)
    d_attend = jnp.einsum("bqhe,bkhe->bhqk", d_mix, value_band, preferred_element_type=jnp.float32)
    inner = jnp.sum(attend * d_attend, axis=-1, keepdims=True)
    d_scores = (attend * (d_attend - inner)).astype(jnp.bfloat16)
    d_value_band = jnp.einsum(
        "bhqk,bqhe->bkhe", attend.astype(jnp.bfloat16), d_mix, preferred_element_type=jnp.float32
    )
    d_query = jnp.einsum(
        "bhqk,bkhe->bqhe", d_scores, key_band, preferred_element_type=jnp.float32
    ) * HEAD ** (-0.5)
    d_key_band = jnp.einsum(
        "bhqk,bqhe->bkhe", d_scores, query_heads, preferred_element_type=jnp.float32
    ) * HEAD ** (-0.5)
    d_key_all = band_back(d_key_band, block_count)
    d_value_all = band_back(d_value_band, block_count)
    stacked = jnp.stack([d_key_all, d_value_all]).reshape(2, block_len + 2 * WIN, D)
    from_below = shifted(stacked[:, block_len + WIN :].astype(jnp.bfloat16), "seq", 1).astype(
        jnp.float32
    )
    from_above = shifted(stacked[:, :WIN].astype(jnp.bfloat16), "seq", -1).astype(jnp.float32)
    middle = stacked[:, WIN : WIN + block_len]
    middle = middle + jnp.pad(from_below, ((0, 0), (0, block_len - WIN), (0, 0)))
    middle = middle + jnp.pad(from_above, ((0, 0), (block_len - WIN, 0), (0, 0)))
    d_key_low = middle[0].astype(jnp.bfloat16)
    d_value_low = middle[1].astype(jnp.bfloat16)
    d_query_low = d_query.reshape(block_len, D).astype(jnp.bfloat16)
    g_w_query = weight_grad(normed, d_query_low)
    g_b_query = jnp.sum(d_query_low.astype(jnp.float32), axis=0)
    g_w_key = weight_grad(normed, d_key_low)
    g_w_value = weight_grad(normed, d_value_low)
    g_b_value = jnp.sum(d_value_low.astype(jnp.float32), axis=0)
    d_normed = (
        input_grad(d_query_low, w_query)
        + input_grad(d_key_low, w_key)
        + input_grad(d_value_low, w_value)
    )
    _, pullback = jax.vjp(
        normalize, source, pre_gain.astype(jnp.float32), pre_shift.astype(jnp.float32)
    )
    d_source, g_pre_gain, g_pre_shift = pullback(d_normed)
    grad_block = d_res + d_source
    grads = (
        g_pre_gain,
        g_pre_shift,
        g_w_query,
        g_b_query,
        g_w_key,
        g_w_value,
        g_b_value,
        g_w_output,
        g_b_output,
        g_mid_gain,
        g_mid_shift,
        g_w_up,
        g_b_up,
        g_w_down,
        g_b_down,
        g_w_conv,
        g_b_conv,
        g_out_gain,
        g_out_shift,
    )
    return (grad_block, grads)


def per_device(
    characters,
    pre_gain,
    pre_shift,
    w_query,
    b_query,
    w_key,
    w_value,
    b_value,
    w_output,
    b_output,
    mid_gain,
    mid_shift,
    w_up,
    b_up,
    w_down,
    b_down,
    w_conv,
    b_conv,
    out_gain,
    out_shift,
    row_lengths,
    row_batch,
    cot_molecules,
):
    shards = (
        pre_gain,
        pre_shift,
        w_query,
        b_query,
        w_key,
        w_value,
        b_value,
        w_output,
        b_output,
        mid_gain,
        mid_shift,
        w_up,
        b_up,
        w_down,
        b_down,
        w_conv,
        b_conv,
        out_gain,
        out_shift,
    )
    seq_count = lax.axis_size("seq")
    seq_place = lax.axis_index("seq")
    block_len = characters.shape[2]
    block_count = block_len // WIN
    buffer_len = block_len * seq_count
    places = seq_place * block_len + jnp.arange(block_len, dtype=jnp.int32)
    band_start = seq_place * block_len - WIN + WIN * jnp.arange(block_count, dtype=jnp.int32)
    key_places = band_start[:, None] + jnp.arange(3 * WIN, dtype=jnp.int32)[None, :]
    flat_keys = key_places.reshape(-1)
    outside = (flat_keys < 0) | (flat_keys >= buffer_len)
    query_blocks = places.reshape(block_count, WIN)
    near = jnp.abs(query_blocks[:, :, None] - key_places[:, None, :]) <= WIN
    lengths = row_lengths[0]
    batches = row_batch[0]
    totals = None
    summed = None
    molecule_list = []
    grad_list = []
    for micro_step in range(characters.shape[0]):
        query_segs = segment_ids(lengths, batches, micro_step, places).reshape(block_count, WIN)
        key_segs = jnp.where(
            outside, -2, segment_ids(lengths, batches, micro_step, flat_keys)
        ).reshape(block_count, 3 * WIN)
        allowed = near & (query_segs[:, :, None] == key_segs[:, None, :])
        weights_all = (
            lax.all_gather(shards[0], ("seq", "dp"), axis=0, tiled=True),
            lax.all_gather(shards[1], ("seq", "dp"), axis=0, tiled=True),
            lax.all_gather(shards[2], ("seq", "dp"), axis=0, tiled=True),
            lax.all_gather(shards[3], ("seq", "dp"), axis=0, tiled=True),
            lax.all_gather(shards[4], ("seq", "dp"), axis=0, tiled=True),
            lax.all_gather(shards[5], ("seq", "dp"), axis=0, tiled=True),
            lax.all_gather(shards[6], ("seq", "dp"), axis=0, tiled=True),
            lax.all_gather(shards[7], ("seq", "dp"), axis=0, tiled=True),
            lax.all_gather(shards[8], ("seq", "dp"), axis=0, tiled=True),
            lax.all_gather(shards[9], ("seq", "dp"), axis=0, tiled=True),
            lax.all_gather(shards[10], ("seq", "dp"), axis=0, tiled=True),
            lax.all_gather(shards[11], ("seq", "dp"), axis=0, tiled=True),
            lax.all_gather(shards[12], ("seq", "dp"), axis=0, tiled=True),
            lax.all_gather(shards[13], ("seq", "dp"), axis=0, tiled=True),
            lax.all_gather(shards[14], ("seq", "dp"), axis=0, tiled=True),
            lax.all_gather(shards[15], ("seq", "dp"), axis=0, tiled=True),
            lax.all_gather(shards[16], ("seq", "dp"), axis=0, tiled=True),
            lax.all_gather(shards[17], ("seq", "dp"), axis=0, tiled=True),
            lax.all_gather(shards[18], ("seq", "dp"), axis=0, tiled=True),
        )
        result, kept = forward(weights_all, characters[micro_step, 0], allowed)
        grad_block, grads = backward(weights_all, kept, cot_molecules[micro_step, 0], allowed)
        molecule_list.append(result)
        grad_list.append(grad_block)
        totals = grads if totals is None else tuple((a + b for a, b in zip(totals, grads)))
    summed = lax.psum_scatter(totals, ("seq", "dp"), scatter_dimension=0, tiled=True)
    molecules = jnp.stack(molecule_list)[:, None]
    grad_chars = jnp.stack(grad_list)[:, None]
    return (molecules, grad_chars) + tuple(summed)


def solution(mesh):
    in_specs = (
        P(None, "dp", "seq", None),
        P(("seq", "dp")),
        P(("seq", "dp")),
        P(("seq", "dp"), None),
        P(("seq", "dp")),
        P(("seq", "dp"), None),
        P(("seq", "dp"), None),
        P(("seq", "dp")),
        P(("seq", "dp"), None),
        P(("seq", "dp")),
        P(("seq", "dp")),
        P(("seq", "dp")),
        P(("seq", "dp"), None),
        P(("seq", "dp")),
        P(("seq", "dp"), None),
        P(("seq", "dp")),
        P(("seq", "dp"), None),
        P(("seq", "dp")),
        P(("seq", "dp")),
        P(("seq", "dp")),
        P("dp", None),
        P("dp", None),
        P(None, "dp", "seq", None),
    )
    out_specs = (
        P(None, "dp", "seq", None),
        P(None, "dp", "seq", None),
        P(("seq", "dp")),
        P(("seq", "dp")),
        P(("seq", "dp"), None),
        P(("seq", "dp")),
        P(("seq", "dp"), None),
        P(("seq", "dp"), None),
        P(("seq", "dp")),
        P(("seq", "dp"), None),
        P(("seq", "dp")),
        P(("seq", "dp")),
        P(("seq", "dp")),
        P(("seq", "dp"), None),
        P(("seq", "dp")),
        P(("seq", "dp"), None),
        P(("seq", "dp")),
        P(("seq", "dp"), None),
        P(("seq", "dp")),
        P(("seq", "dp")),
        P(("seq", "dp")),
    )
    return jax.shard_map(
        per_device, mesh=mesh, in_specs=in_specs, out_specs=out_specs, check_vma=False
    )
```

profile of v0, /device:TPU:0, one launch (start us, length us, event | category | flops | bytes accessed | tf_op | source)
XLA Modules:
  0.0 1390.5 jit_solution(17023620456325846326)
XLA Ops:
  20.1 42.5 %all-reduce.45 = (bf16[768]{0:T(1024)(128)(2,1)S(1)}, bf16[768]{0:T(1024)(128)(2,1)S(1)}, bf16[768]{0:T(1024)(128)(2,1)S(1)}, bf16[768]{0:T(1024)(128)(2,1)S(1)}...) all-reduce(bf16[768]{0:T(1024)(128)(2,1)S(1)} %dynamic-update-slice, ...), channel_id=1, replica_groups=mesh['seq'=2,'dp'=16] {'seq','dp'}, use_global_device_ids=true, to_apply=%add.30 | all-reduce | flops 11520 | bytes 46080
  75.0 48.8 %all-gather.8.cloned.1.call-done = bf16[768,768]{1,0:T(8,128)(2,1)} async-done(((bf16[24,768]{1,0:T(8,128)(2,1)}), bf16[768,768]{1,0:T(8,128)(2,1)}) %all-gather.8.cloned.1.call-update) | async-done | bytes 1179664 | tf_op jit(solution)/shard_map/all_gather | solution.py:385
  126.0 53.7 %all-gather.10.cloned.1.call-done = bf16[768,768]{1,0:T(8,128)(2,1)} async-done(((bf16[24,768]{1,0:T(8,128)(2,1)}), bf16[768,768]{1,0:T(8,128)(2,1)}) %all-gather.10.cloned.1.call-update) | async-done | bytes 1179664 | tf_op jit(solution)/shard_map/all_gather | solution.py:386
  209.9 8.3 fusion.232
  243.5 5.8 fusion.87
  269.3 31.5 %all-gather.16.cloned.1.call-done = bf16[768,3072]{1,0:T(8,128)(2,1)} async-done(((bf16[24,3072]{1,0:T(8,128)(2,1)}), bf16[768,3072]{1,0:T(8,128)(2,1)}) %all-gather.16.cloned.1.call-update) | async-done | bytes 4718608 | tf_op jit(solution)/shard_map/all_gather | solution.py:392
  300.8 8.2 fusion.206
  309.0 56.9 %all-gather.18.cloned.1.call-done = bf16[3072,768]{1,0:T(8,128)(2,1)} async-done(((bf16[96,768]{1,0:T(8,128)(2,1)}), bf16[3072,768]{1,0:T(8,128)(2,1)}) %all-gather.18.cloned.1.call-update) | async-done | bytes 4718608 | tf_op jit(solution)/shard_map/all_gather | solution.py:394
  366.0 9.5 add_convert_fusion.4
  377.9 53.3 %all-gather.20.cloned.1.call-done = bf16[3072,768]{1,0:T(8,128)(2,1)} async-done(((bf16[96,768]{1,0:T(8,128)(2,1)}), bf16[3072,768]{1,0:T(8,128)(2,1)}) %all-gather.20.cloned.1.call-update) | async-done | bytes 4718608 | tf_op jit(solution)/shard_map/all_gather | solution.py:396
  469.7 10.1 fusion.235
  479.8 10.7 fusion.234
  508.5 8.1 fusion.35
  516.6 6.4 multiply_reduce_fusion
  576.1 8.0 fusion.32
  620.3 6.6 fusion.158
  627.0 10.5 convolution_add_fusion.1
  670.5 41.1 %all-reduce.44 = (f32[768]{0:T(1024)S(1)}, f32[768]{0:T(1024)S(1)}, f32[768]{0:T(1024)S(1)}, f32[768]{0:T(1024)S(1)}, f32[768]{0:T(1024)S(1)}, /*index=5*/f32[76...) all-reduce(f32[768]{0:T(1024)S(1)} %add.676, ...), channel_id=2, replica_groups=mesh['seq'=2,'dp'=16] {'seq','dp'}, use_global_device_ids=true, to_apply=%region_37.38.clone | all-reduce | flops 11520 | bytes 92160
  723.5 27.4 %reduce-scatter.8.cloned.1.call-done = f32[24,768]{1,0:T(8,128)} async-done(((f32[768,768]{1,0:T(8,128)}), f32[24,768]{1,0:T(8,128)}) %reduce-scatter.8.cloned.1.call-update) | async-done | bytes 73744 | tf_op jit(solution)/shard_map/reduce_scatter | solution.py:406
  750.9 103.9 %reduce-scatter.12.cloned.1.call-done = f32[24,768]{1,0:T(8,128)} async-done(((f32[768,768]{1,0:T(8,128)}), f32[24,768]{1,0:T(8,128)}) %reduce-scatter.12.cloned.1.call-update) | async-done | bytes 73744 | tf_op jit(solution)/shard_map/reduce_scatter | solution.py:406
  854.8 104.8 %reduce-scatter.10.cloned.1.call-done = f32[24,768]{1,0:T(8,128)} async-done(((f32[768,768]{1,0:T(8,128)}), f32[24,768]{1,0:T(8,128)}) %reduce-scatter.10.cloned.1.call-update) | async-done | bytes 73744 | tf_op jit(solution)/shard_map/reduce_scatter | solution.py:406
  959.6 141.1 %reduce-scatter.18.cloned.1.call-done = f32[96,768]{1,0:T(8,128)} async-done(((f32[3072,768]{1,0:T(8,128)}), f32[96,768]{1,0:T(8,128)}) %reduce-scatter.18.cloned.1.call-update) | async-done | bytes 294928 | tf_op jit(solution)/shard_map/reduce_scatter | solution.py:406
  1100.7 141.9 %reduce-scatter.16.cloned.1.call-done = f32[24,3072]{1,0:T(8,128)} async-done(((f32[768,3072]{1,0:T(8,128)}), f32[24,3072]{1,0:T(8,128)}) %reduce-scatter.16.cloned.1.call-update) | async-done | bytes 294928 | tf_op jit(solution)/shard_map/reduce_scatter | solution.py:406
  1242.5 141.2 %reduce-scatter.20.cloned.1.call-done = f32[96,768]{1,0:T(8,128)} async-done(((f32[3072,768]{1,0:T(8,128)}), f32[96,768]{1,0:T(8,128)}) %reduce-scatter.20.cloned.1.call-update) | async-done | bytes 294928 | tf_op jit(solution)/shard_map/reduce_scatter | solution.py:406
  (629 shorter events, 293.4 us)
Async XLA Ops:
  7.2 60.7 %all-gather.12.cloned.1.call-start = ((), (), s32[]{:S(2)}) async-start(), calls=%async_computation.9 | async-start | bytes 1216512 | tf_op jit(solution)/shard_map/all_gather | solution.py:383
  7.9 115.9 %all-gather.8.cloned.1.call-start = ((), (), s32[]{:S(2)}) async-start(), calls=%async_computation.7 | async-start | bytes 1216512 | tf_op jit(solution)/shard_map/all_gather | solution.py:385
  8.7 171.1 %all-gather.10.cloned.1.call-start = ((), (), s32[]{:S(2)}) async-start(), calls=%async_computation.8 | async-start | bytes 1216512 | tf_op jit(solution)/shard_map/all_gather | solution.py:386
  9.4 252.5 %all-gather.14.cloned.1.call-start = ((), (), s32[]{:S(2)}) async-start(), calls=%async_computation.10 | async-start | bytes 1216512 | tf_op jit(solution)/shard_map/all_gather | solution.py:388
  10.0 290.9 %all-gather.16.cloned.1.call-start = ((), (), s32[]{:S(2)}) async-start(), calls=%async_computation.11 | async-start | bytes 4866048 | tf_op jit(solution)/shard_map/all_gather | solution.py:392
  10.6 355.4 %all-gather.18.cloned.1.call-start = ((), (), s32[]{:S(2)}) async-start(), calls=%async_computation.12 | async-start | bytes 4866048 | tf_op jit(solution)/shard_map/all_gather | solution.py:394
  11.2 420.1 %all-gather.20.cloned.1.call-start = ((), (), s32[]{:S(2)}) async-start(), calls=%async_computation.13 | async-start | bytes 4866048 | tf_op jit(solution)/shard_map/all_gather | solution.py:396
  11.9 711.6 %reduce-scatter.14.cloned.1.call-start = ((), (), s32[]{:S(2)}) async-start(), calls=%async_computation.17 | async-start | bytes 2433024 | tf_op jit(solution)/shard_map/reduce_scatter | solution.py:406
  62.7 372.7 %copy-start.96 = (f32[768]{0:T(1024)}, f32[768]{0:T(1024)S(1)}, u32[]{:S(2)}) copy-start(f32[768]{0:T(1024)S(1)} %convert_element_type.328) | copy-start | bytes 9220
  182.0 13.9 collective-permute-start
  185.5 13.5 collective-permute-start.1
  189.8 28.4 %collective-permute-start.2 = (bf16[2,128,768]{2,1,0:T(8,128)(2,1)}, bf16[2,128,768]{2,1,0:T(8,128)(2,1)S(1)}, u32[]{:S(2)}, u32[]{:S(2)}) collective-permute-start(bf16[2,128,768]{2,1,0:T(8,128)(2,1)} %get-tuple-element.211), channel_id=1, source_target_pairs={{0,16},{1,17},{2,18},{3,19},{4,20},{5,21},{6,22},{7,23},{8,24},{9,... | collective-permute-start | bytes 1179656 | tf_op jit(solution)/shard_map/ppermute | solution.py:23
  194.4 23.8 %collective-permute-start.3 = (bf16[2,128,768]{2,1,0:T(8,128)(2,1)}, bf16[2,128,768]{2,1,0:T(8,128)(2,1)}, u32[]{:S(2)}, u32[]{:S(2)}) collective-permute-start(bf16[2,128,768]{2,1,0:T(8,128)(2,1)} %get-tuple-element.212), channel_id=1, source_target_pairs={{16,0},{17,1},{18,2},{19,3},{20,4},{21,5},{22,6},{23,7},{24,8},{25... | collective-permute-start | bytes 1179656 | tf_op jit(solution)/shard_map/ppermute | solution.py:24
  267.0 230.4 %copy-start.102 = (f32[512]{0:T(512)}, f32[512]{0:T(512)S(1)}, u32[]{:S(2)}) copy-start(f32[512]{0:T(512)S(1)} %broadcast_multiply_fusion) | copy-start | bytes 6148
  546.7 204.2 %reduce-scatter.8.cloned.1.call-start = ((), (), s32[]{:S(2)}) async-start(), calls=%async_computation.14 | async-start | bytes 2433024 | tf_op jit(solution)/shard_map/reduce_scatter | solution.py:406
  557.2 42.8 %collective-permute-start.6 = (bf16[2,128,768]{1,2,0:T(8,128)(2,1)}, bf16[2,128,768]{1,2,0:T(8,128)(2,1)}, u32[]{:S(2)}, u32[]{:S(2)}) collective-permute-start(bf16[2,128,768]{1,2,0:T(8,128)(2,1)} %get-tuple-element.193), channel_id=1, source_target_pairs={{0,16},{1,17},{2,18},{3,19},{4,20},{5,21},{6,22},{7,23},{8,24},{9,... | collective-permute-start | bytes 1179656 | tf_op jit(solution)/shard_map/ppermute | solution.py:32
  561.6 38.4 %collective-permute-start.7 = (bf16[2,128,768]{1,2,0:T(8,128)(2,1)}, bf16[2,128,768]{1,2,0:T(8,128)(2,1)}, u32[]{:S(2)}, u32[]{:S(2)}) collective-permute-start(bf16[2,128,768]{1,2,0:T(8,128)(2,1)} %get-tuple-element.194), channel_id=1, source_target_pairs={{16,0},{17,1},{18,2},{19,3},{20,4},{21,5},{22,6},{23,7},{24,8},{25... | collective-permute-start | bytes 1179656 | tf_op jit(solution)/shard_map/ppermute | solution.py:32
  584.2 270.6 %reduce-scatter.12.cloned.1.call-start = ((), (), s32[]{:S(2)}) async-start(), calls=%async_computation.16 | async-start | bytes 2433024 | tf_op jit(solution)/shard_map/reduce_scatter | solution.py:406
  593.1 13.7 collective-permute-start.4
  598.7 12.3 collective-permute-start.5
  614.9 344.6 %reduce-scatter.10.cloned.1.call-start = ((), (), s32[]{:S(2)}) async-start(), calls=%async_computation.15 | async-start | bytes 2433024 | tf_op jit(solution)/shard_map/reduce_scatter | solution.py:406
  619.9 480.8 %reduce-scatter.18.cloned.1.call-start = ((), (), s32[]{:S(2)}) async-start(), calls=%async_computation.19 | async-start | bytes 9732096 | tf_op jit(solution)/shard_map/reduce_scatter | solution.py:406
  637.5 605.0 %reduce-scatter.16.cloned.1.call-start = ((), (), s32[]{:S(2)}) async-start(), calls=%async_computation.18 | async-start | bytes 9732096 | tf_op jit(solution)/shard_map/reduce_scatter | solution.py:406
  649.3 734.4 %reduce-scatter.20.cloned.1.call-start = ((), (), s32[]{:S(2)}) async-start(), calls=%async_computation.20 | async-start | bytes 9732096 | tf_op jit(solution)/shard_map/reduce_scatter | solution.py:406
  (179 other events, 2200.5 us)
Sparse Core Ops, SparseCore 0:
  10.9 56.8 all-gather.11
  70.8 52.9 all-gather.7
  126.7 52.9 all-gather.9
  182.5 53.0 all-gather.13
  238.3 62.4 all-gather.15
  303.6 62.3 all-gather.17
  368.9 62.3 all-gather.19
  546.8 99.1 reduce-scatter.13
  652.7 98.1 reduce-scatter.7
  756.6 98.1 reduce-scatter.11
  861.5 98.0 reduce-scatter.9
  965.9 134.7 reduce-scatter.17
  1108.1 134.3 reduce-scatter.15
  1248.8 134.8 reduce-scatter.19
where the time goes:
time: 1400 us; the launch traced here: 1390 us
  waiting for transfers between devices  923 us (66%)
  matrix products  205 us (15%)
  local copies, waits for them, and re-layouts  86.6 us (6%)
  blocking collectives  83.6 us (6%)
  other arithmetic  50.4 us (4%)
  starting transfers between devices  25 us (2%)
  between operations  16.8 us (1%)
    reduce_scatter x7, waiting for transfers between devices, per_device(): lax.psum_scatter(totals, ('seq', 'dp'), scatter_dimension=0, tiled=True)  660 us
    unnamed x2, blocking collectives  83.6 us
    all_gather x1, waiting for transfers between devices, per_device(): lax.all_gather(shards[13], ('seq', 'dp'), axis=0, tiled=True)  56.9 us
    all_gather x1, waiting for transfers between devices, per_device(): lax.all_gather(shards[5], ('seq', 'dp'), axis=0, tiled=True)  53.7 us
    dot_general x14, matrix products, weight_grad(): lax.dot_general(left, right, (((0,), (0,)), ((), ())), preferred_element_...  53.4 us
    all_gather x1, waiting for transfers between devices, per_device(): lax.all_gather(shards[15], ('seq', 'dp'), axis=0, tiled=True)  53.3 us
    all_gather x1, waiting for transfers between devices, per_device(): lax.all_gather(shards[4], ('seq', 'dp'), axis=0, tiled=True)  48.8 us
    dot_general x14, matrix products, forward_dot(): return jnp.dot(left, right, preferred_element_type=jnp.float32)  46.4 us
  transfers between devices with their start and end apart: 22, of which 15 were waited for; matrix products, arithmetic and copies ran while one was open for 16% of the time, Pallas kernels for 0%

commit v1 on v0

v1 whole, which is shorter than its diff:
```python
import functools

import jax
import jax.numpy as jnp
from jax import lax
from jax.experimental import pallas as pl
from jax.experimental.pallas import tpu as pltpu
from jax.sharding import PartitionSpec as P

D = 768
HEADS = 12
HEAD = 64
KER = 4
WIN = 128
EPSILON = 1e-05
MESH = pl.DeviceIdType.MESH
AXES = ("seq", "dp")
F32 = jnp.float32
BF16 = jnp.bfloat16


def normalize(vector, gain, shift):
    average = jnp.mean(vector, axis=-1, keepdims=True)
    centered = vector - average
    variance = jnp.mean(centered * centered, axis=-1, keepdims=True)
    return centered * lax.rsqrt(variance + EPSILON) * gain + shift


def segment_ids(lengths, batches, micro_step, places):
    slot_ids = jnp.arange(lengths.shape[0], dtype=jnp.int32)
    before = (slot_ids[:, None] < slot_ids[None, :]) & (batches[:, None] == batches[None, :])
    starts = jnp.sum(jnp.where(before, lengths[:, None], 0), axis=0)
    inside = (
        (batches[:, None] == micro_step)
        & (places[None, :] >= starts[:, None])
        & (places[None, :] < (starts + lengths)[:, None])
    )
    return jnp.sum(jnp.where(inside, slot_ids[:, None] + 1, 0), axis=0) - 1


def forward_dot(left, right):
    return jnp.dot(left, right, preferred_element_type=F32)


def weight_grad(left, right):
    return lax.dot_general(left, right, (((0,), (0,)), ((), ())), preferred_element_type=F32)


def input_grad(left, weight):
    return lax.dot_general(left, weight, (((1,), (1,)), ((), ())), preferred_element_type=F32)


class Place:
    def __init__(self, nz):
        self.nz = nz
        dp = lax.axis_index("dp")
        self.x = lax.axis_index("seq")
        self.core = lax.rem(dp, 2)
        self.y = lax.rem(dp // 2, 2)
        self.z = dp // 4

    def device(self, x=None, z=None, y=None, core=None):
        x = self.x if x is None else x
        z = self.z if z is None else z
        y = self.y if y is None else y
        core = self.core if core is None else core
        return (x, z * 4 + y * 2 + core)

    def partner(self):
        return self.device(core=1 - self.core)

    def across_x(self):
        return self.device(x=1 - self.x)

    def across_y(self):
        return self.device(y=1 - self.y)

    def z_ahead(self, offset):
        return lax.rem(self.z + offset, self.nz)

    def along_z(self, offset):
        return self.device(z=self.z_ahead(offset))


def greet(place):
    barrier = pltpu.get_barrier_semaphore()
    others = [place.partner(), place.across_x(), place.across_y()]
    others += [place.along_z(o) for o in range(1, place.nz)]
    for other in others:
        pl.semaphore_signal(barrier, inc=1, device_id=other, device_id_type=MESH)
    pl.semaphore_wait(barrier, len(others))


class Sender:
    def __init__(self, send_sems, recv_sems):
        self.send_sems, self.recv_sems = send_sems, recv_sems
        self.count = 0
        self.open = []

    def start(self, src, dst, device):
        copy = pltpu.make_async_remote_copy(
            src_ref=src,
            dst_ref=dst,
            send_sem=self.send_sems.at[self.count],
            recv_sem=self.recv_sems.at[self.count],
            device_id=device,
            device_id_type=MESH,
        )
        self.count += 1
        copy.start()
        self.open.append(copy)
        return copy

    def finish(self):
        for copy in self.open:
            copy.wait_send()


def gather_kernel(
    nz, wq, wk, wv, wo, wu, wd, wc, vec, w1, w2, vecs, own, pre, slab, vpair, send_sems, recv_sems, sems
):
    place = Place(nz)
    x, y, z, core = place.x, place.y, place.z, place.core
    sender = Sender(send_sems, recv_sems)
    for m, ref in enumerate((wq, wk, wv, wo)):
        own[m % 2, m // 2] = ref[...]
    for j in range(4):
        own[j % 2, 2 + j // 2] = wu[:, j * D : (j + 1) * D]
    for t in range(4):
        pre[core, t] = own[core, t]
    vpair[core] = vec[...]
    local = [
        pltpu.make_async_copy(wd, w2.at[0, x, z, y, core], sems.at[0]),
        pltpu.make_async_copy(wc, w2.at[1, x, z, y, core], sems.at[1]),
    ]
    for copy in local:
        copy.start()
    greet(place)
    swap = sender.start(own.at[1 - core], pre.at[core], place.partner())
    vswap = sender.start(vec, vpair.at[core], place.partner())
    swap.wait_recv()
    vswap.wait_recv()
    for t in range(4):
        both = [pre[i, t].astype(F32) for i in range(2)]
        slab[t] = jnp.concatenate(both, axis=0).astype(BF16)
    mine = [
        pltpu.make_async_copy(slab, w1.at[:, core, x, z, y], sems.at[2]),
        pltpu.make_async_copy(vpair, vecs.at[x, z, y], sems.at[3]),
    ]
    for copy in mine:
        copy.start()
    local += mine

    def z_block(p):
        if p < 2:
            return slab.at[pl.ds(2 * p, 2)], w1.at[pl.ds(2 * p, 2), core, x, z, y]
        return (wd, wc)[p - 2], w2.at[p - 2, x, z, y, core]

    def send_z(p):
        src, dst = z_block(p)
        copies = [sender.start(src, dst, place.along_z(o)) for o in range(1, nz)]
        if p == 0:
            dst = vecs.at[x, z, y]
            copies += [sender.start(vpair, dst, place.along_z(o)) for o in range(1, nz)]
        return copies

    def send_first(p):
        if p < 2:
            a, b = w1.at[2 * p, core, x, :, y], w1.at[2 * p + 1, core, x, :, y]
        else:
            a, b = w2.at[p - 2, x, :, y, core, 0], w2.at[p - 2, x, :, y, core, 1]
        copies = [sender.start(a, a, place.across_x()), sender.start(b, b, place.across_y())]
        if p == 0:
            v = vecs.at[x, :, y]
            copies.append(sender.start(v, v, place.across_x()))
        return copies

    def send_second(p):
        if p < 2:
            a, b = w1.at[2 * p, core, :, :, y], w1.at[2 * p + 1, core, x]
        else:
            a, b = w2.at[p - 2, :, :, y, core, 0], w2.at[p - 2, x, :, :, core, 1]
        copies = [sender.start(a, a, place.across_y()), sender.start(b, b, place.across_x())]
        if p == 0:
            v = vecs.at[:, :, y]
            copies.append(sender.start(v, v, place.across_y()))
        return copies

    def send_core(p):
        ref = w1.at[pl.ds(2 * p, 2), core] if p < 2 else w2.at[p - 2, :, :, :, core]
        return [sender.start(ref, ref, place.partner())]

    stages = (send_z, send_first, send_second, send_core)
    going = {}
    for step in range(4 + len(stages)):
        for stage in reversed(range(len(stages))):
            p = step - stage
            if 0 <= p < 4:
                if stage > 0:
                    for copy in going[stage - 1, p]:
                        copy.wait_recv()
                if stage == 1 and p == 0:
                    for copy in local:
                        copy.wait()
                going[stage, p] = stages[stage](p)
        p = step - len(stages)
        if 0 <= p < 4:
            for copy in going[len(stages) - 1, p]:
                copy.wait_recv()
    sender.finish()


def gather_weights(nz, mats, vec):
    rows = mats[0].shape[0]
    any_spec = pl.BlockSpec(memory_space=pl.ANY)
    vmem = pl.BlockSpec(memory_space=pltpu.VMEM)
    wd, wc = (w.reshape(2, 2 * rows, D) for w in mats[5:])
    copies = 2 + 4 * (nz - 1 + 2 + 2 + 1) + (nz - 1 + 2)
    return pl.pallas_call(
        functools.partial(gather_kernel, nz),
        out_shape=(
            jax.ShapeDtypeStruct((4, 2, 2, nz, 2, 2 * rows, D), BF16),
            jax.ShapeDtypeStruct((2, 2, nz, 2, 2, 2, 2 * rows, D), BF16),
            jax.ShapeDtypeStruct((2, nz, 2, 2, 16, 128), BF16),
        ),
        in_specs=[vmem] * 5 + [any_spec] * 2 + [vmem],
        out_specs=(any_spec,) * 3,
        scratch_shapes=[
            pltpu.VMEM((2, 4, rows, D), BF16),
            pltpu.VMEM((2, 4, rows, D), BF16),
            pltpu.VMEM((4, 2 * rows, D), BF16),
            pltpu.VMEM((2, 16, 128), BF16),
            pltpu.SemaphoreType.DMA((copies,)),
            pltpu.SemaphoreType.DMA((copies,)),
            pltpu.SemaphoreType.DMA((4,)),
        ],
        compiler_params=pltpu.CompilerParams(
            collective_id=1, has_side_effects=True, vmem_limit_bytes=24 << 20
        ),
        name="gather_weights",
    )(*mats[:5], wd, wc, vec)


def add_into(dst, a, b, count):
    def body(i, carry):
        dst(i)[...] = (a(i)[...].astype(F32) + b(i)[...].astype(F32)).astype(BF16)
        return carry

    lax.fori_loop(0, count, body, 0)


def scatter_kernel(
    nz,
    g1,
    g2,
    gv,
    out1,
    out2,
    outv,
    own1,
    own2,
    rc1,
    rc2,
    half1,
    half2,
    quarter,
    rz,
    fin,
    vown,
    vrc,
    vhalf,
    vquarter,
    vrz,
    send_sems,
    recv_sems,
    sems,
):
    place = Place(nz)
    x, y, z, core = place.x, place.y, place.z, place.core
    sender = Sender(send_sems, recv_sems)
    pieces = (3, 2, 1, 0)

    def full(p):
        return g1.at[pl.ds(2 * p, 2)] if p < 2 else g2.at[p - 2]

    def part(ref, p, which):
        if p < 2:
            return [ref.at[2 * p + i, which] for i in range(2)]
        return [ref.at[p - 2, :, :, :, which, i] for i in range(2)]

    def box(ref1, ref2, p, i):
        return ref1.at[2 * p + i] if p < 2 else ref2.at[p - 2, i]

    local = {}
    for n, p in enumerate(pieces):
        local[p] = []
        for i in range(2):
            copy = pltpu.make_async_copy(part((g1, g2)[p >= 2], p, core)[i], box(own1, own2, p, i), sems.at[2 * n + i])
            copy.start()
            local[p].append(copy)
    vlocal = pltpu.make_async_copy(gv.at[:, :, :, core], vown, sems.at[8])
    vlocal.start()
    greet(place)
    going = {}

    def send_core(p):
        src = part((g1, g2)[p >= 2], p, 1 - core)
        copies = [sender.start(src[i], box(rc1, rc2, p, i), place.partner()) for i in range(2)]
        if p == 0:
            copies.append(sender.start(gv.at[:, :, :, 1 - core], vrc, place.partner()))
        return copies

    def send_first(p):
        for copy in local[p]:
            copy.wait()
        copies = []
        for i in range(2):
            own, got = box(own1, own2, p, i), box(rc1, rc2, p, i)

            def at(ref, side, i=i):
                if i == 0:
                    return lambda n: ref.at[n // nz, lax.rem(n, nz), side]
                return lambda n: ref.at[side, n // 2, lax.rem(n, 2)]

            there, here = (1 - y, y) if i == 0 else (1 - x, x)
            add_into(at(own, there), at(own, there), at(got, there), 2 * nz)
            src = own.at[:, :, there] if i == 0 else own.at[there]
            to = place.across_y() if i == 0 else place.across_x()
            dst = half1.at[p] if i == 0 else half2.at[p]
            copies.append(sender.start(src, dst, to))
            add_into(at(own, here), at(own, here), at(got, here), 2 * nz)
        if p == 0:
            vlocal.wait()
            vown[...] = vown[...] + vrc[...]
            copies.append(sender.start(vown.at[:, :, 1 - y], vhalf, place.across_y()))
        return copies

    def send_second(p):
        copies = []
        for i in range(2):
            own = box(own1, own2, p, i)
            if i == 0:
                got = half1.at[p]

                def mine(side):
                    return lambda n: own.at[side, n, y]

                def theirs(side):
                    return lambda n: got.at[side, n]

                there, here = 1 - x, x
                src = own.at[there, :, y]
                to = place.across_x()
            else:
                got = half2.at[p]

                def mine(side):
                    return lambda n: own.at[x, n, side]

                def theirs(side):
                    return lambda n: got.at[n, side]

                there, here = 1 - y, y
                src = own.at[x, :, there]
                to = place.across_y()
            add_into(mine(there), mine(there), theirs(there), nz)
            copies.append(sender.start(src, quarter.at[p, i], to))
            add_into(mine(here), mine(here), theirs(here), nz)
        if p == 0:
            for n in range(2):
                vown[n, :, y] = vown[n, :, y] + vhalf[n]
            copies.append(sender.start(vown.at[1 - x, :, y], vquarter, place.across_x()))
        return copies

    def send_z(p):
        copies = []
        for i in range(2):
            own = box(own1, own2, p, i)

            def mine(n):
                return own.at[x, n, y]

            add_into(mine, mine, lambda n: quarter.at[p, i, n], nz)
            for o in range(1, nz):
                copies.append(sender.start(mine(place.z_ahead(o)), rz.at[p, i, o - 1], place.along_z(o)))
        if p == 0:
            vown[x, :, y] = vown[x, :, y] + vquarter[...]
            for o in range(1, nz):
                src = vown.at[x, place.z_ahead(o), y]
                copies.append(sender.start(src, vrz.at[o - 1], place.along_z(o)))
        return copies

    def finish(p):
        for i in range(2):
            own = box(own1, own2, p, i)
            total = own[x, z, y].astype(F32)
            for o in range(1, nz):
                total = total + rz[p, i, o - 1].astype(F32)
            if p < 2:
                rows = total.shape[0] // 2
                fin[2 * p + i, 0] = total[:rows]
                fin[2 * p + i, 1] = total[rows:]
                out1[2 * p + i, core] = fin[2 * p + i, core]
            else:
                out2[p - 2, i] = total
        if p == 0:
            total = vown[x, z, y]
            for o in range(1, nz):
                total = total + vrz[o - 1]
            outv[...] = total
        if p < 2:
            t = pl.ds(2 * p, 2)
            return [sender.start(fin.at[t, 1 - core], out1.at[t, core], place.partner())]
        return []

    stages = (send_core, send_first, send_second, send_z, finish)
    last = []
    for step in range(4 + len(stages) - 1):
        for stage in range(len(stages)):
            n = step - stage
            if 0 <= n < 4:
                p = pieces[n]
                if stage > 0:
                    for copy in going[stage - 1, p]:
                        copy.wait_recv()
                going[stage, p] = stages[stage](p)
                if stage == len(stages) - 1:
                    last += going[stage, p]
    for copy in last:
        copy.wait_recv()
    sender.finish()


def scatter_grads(nz, rows2, g1, g2, gv):
    any_spec = pl.BlockSpec(memory_space=pl.ANY)
    vmem = pl.BlockSpec(memory_space=pltpu.VMEM)
    copies = 4 * (2 + 2 + 2 + 2 * (nz - 1)) + 3 + nz - 1 + 2
    return pl.pallas_call(
        functools.partial(scatter_kernel, nz),
        out_shape=(
            jax.ShapeDtypeStruct((4, 2, rows2 // 2, D), F32),
            jax.ShapeDtypeStruct((2, 2, rows2, D), F32),
            jax.ShapeDtypeStruct((16, 128), F32),
        ),
        in_specs=[any_spec] * 3,
        out_specs=(vmem,) * 3,
        scratch_shapes=[
            pltpu.VMEM((4, 2, nz, 2, rows2, D), BF16),
            pltpu.VMEM((2, 2, 2, nz, 2, rows2, D), BF16),
            pltpu.VMEM((4, 2, nz, 2, rows2, D), BF16),
            pltpu.VMEM((2, 2, 2, nz, 2, rows2, D), BF16),
            pltpu.VMEM((4, 2, nz, rows2, D), BF16),
            pltpu.VMEM((4, nz, 2, rows2, D), BF16),
            pltpu.VMEM((4, 2, nz, rows2, D), BF16),
            pltpu.VMEM((4, 2, nz - 1, rows2, D), BF16),
            pltpu.VMEM((4, 2, rows2 // 2, D), F32),
            pltpu.VMEM((2, nz, 2, 16, 128), F32),
            pltpu.VMEM((2, nz, 2, 16, 128), F32),
            pltpu.VMEM((2, nz, 16, 128), F32),
            pltpu.VMEM((nz, 16, 128), F32),
            pltpu.VMEM((nz - 1, 16, 128), F32),
            pltpu.SemaphoreType.DMA((copies,)),
            pltpu.SemaphoreType.DMA((copies,)),
            pltpu.SemaphoreType.DMA((9,)),
        ],
        compiler_params=pltpu.CompilerParams(
            collective_id=2, has_side_effects=True, vmem_limit_bytes=56 << 20
        ),
        name="scatter_grads",
    )(g1, g2, gv)


def band_rows(rows_all, block_count):
    return jnp.stack([rows_all[b * WIN : b * WIN + 3 * WIN] for b in range(block_count)])


def band_back(band_grads, block_count):
    total = None
    for b in range(block_count):
        padded = jnp.pad(band_grads[b], ((b * WIN, (block_count - 1 - b) * WIN), (0, 0), (0, 0)))
        total = padded if total is None else total + padded
    return total


def shifted(value, axis, steps):
    count = lax.axis_size(axis)
    initial, last = (max(0, -steps), min(count, count - steps))
    return lax.ppermute(value, axis, [(source, source + steps) for source in range(initial, last)])


def with_halo(x, width, dim):
    length = x.shape[dim]
    last = lax.slice_in_dim(x, length - width, length, axis=dim)
    initial = lax.slice_in_dim(x, 0, width, axis=dim)
    return jnp.concatenate([shifted(last, "seq", 1), x, shifted(initial, "seq", -1)], axis=dim)


def layer(mats, vecs, chars, cot, allowed):
    w_query, w_key, w_value, w_output, w_up, w_down, w_conv = mats
    v = {name: value.astype(F32) for name, value in vecs.items()}
    micro, block_len, _ = chars.shape
    count = block_len // WIN
    rows = micro * block_len
    source = chars.astype(F32).reshape(rows, D)
    normed = normalize(source, v["pre_gain"], v["pre_shift"]).astype(BF16)
    queries = (forward_dot(normed, w_query) + v["b_query"]).astype(BF16)
    key_rows = forward_dot(normed, w_key).astype(BF16)
    value_rows = (forward_dot(normed, w_value) + v["b_value"]).astype(BF16)
    stacked = jnp.stack([key_rows, value_rows]).reshape(2, micro, block_len, D)
    stacked = with_halo(stacked, WIN, 2)
    heads = stacked.reshape(2, micro, block_len + 2 * WIN, HEADS, HEAD)
    query_heads = queries.reshape(micro * count, WIN, HEADS, HEAD)
    key_band = jnp.concatenate([band_rows(heads[0, m], count) for m in range(micro)])
    value_band = jnp.concatenate([band_rows(heads[1, m], count) for m in range(micro)])
    scores = jnp.einsum("bqhe,bkhe->bhqk", query_heads, key_band, preferred_element_type=F32) * HEAD ** (-0.5)
    allowed = allowed.reshape(micro * count, 1, WIN, 3 * WIN)
    scores = jnp.where(allowed, scores, -1e30)
    largest = jnp.max(scores, axis=-1, keepdims=True)
    powers = jnp.exp(scores - largest)
    norm_sum = jnp.sum(powers, axis=-1, keepdims=True)
    attend = powers / norm_sum
    attend_low = attend.astype(BF16)
    mixture = jnp.einsum("bhqk,bkhe->bqhe", attend_low, value_band, preferred_element_type=F32)
    mixture = mixture.reshape(rows, D).astype(BF16)
    residual = source + (forward_dot(mixture, w_output) + v["b_output"])
    normed2 = normalize(residual, v["mid_gain"], v["mid_shift"]).astype(BF16)
    hidden = forward_dot(normed2, w_up) + v["b_up"]
    active = jax.nn.gelu(hidden).astype(BF16)
    residual2 = residual + (forward_dot(active, w_down) + v["b_down"])
    grouped = residual2.astype(BF16).reshape(rows // KER, KER * D)
    conv_out = forward_dot(grouped, w_conv) + v["b_conv"]
    curved = jax.nn.gelu(conv_out)
    result = normalize(curved, v["out_gain"], v["out_shift"]).astype(BF16)

    g = {}
    _, pullback = jax.vjp(normalize, curved, v["out_gain"], v["out_shift"])
    d_curved, g["out_gain"], g["out_shift"] = pullback(cot.astype(F32).reshape(rows // KER, D))
    _, pullback = jax.vjp(jax.nn.gelu, conv_out)
    (d_conv,) = pullback(d_curved)
    g["b_conv"] = jnp.sum(d_conv, axis=0)
    d_conv_low = d_conv.astype(BF16)
    g["w_conv"] = weight_grad(grouped, d_conv_low)
    d_res2 = input_grad(d_conv_low, w_conv).reshape(rows, D)
    g["b_down"] = jnp.sum(d_res2, axis=0)
    d_res2_low = d_res2.astype(BF16)
    g["w_down"] = weight_grad(active, d_res2_low)
    d_active = input_grad(d_res2_low, w_down)
    _, pullback = jax.vjp(jax.nn.gelu, hidden)
    (d_hidden,) = pullback(d_active)
    g["b_up"] = jnp.sum(d_hidden, axis=0)
    d_hidden_low = d_hidden.astype(BF16)
    g["w_up"] = weight_grad(normed2, d_hidden_low)
    d_normed2 = input_grad(d_hidden_low, w_up)
    _, pullback = jax.vjp(normalize, residual, v["mid_gain"], v["mid_shift"])
    d_middle, g["mid_gain"], g["mid_shift"] = pullback(d_normed2)
    d_res = d_res2 + d_middle
    g["b_output"] = jnp.sum(d_res, axis=0)
    d_res_low = d_res.astype(BF16)
    g["w_output"] = weight_grad(mixture, d_res_low)
    d_mix = input_grad(d_res_low, w_output).astype(BF16).reshape(micro * count, WIN, HEADS, HEAD)
    d_attend = jnp.einsum("bqhe,bkhe->bhqk", d_mix, value_band, preferred_element_type=F32)
    inner = jnp.sum(attend * d_attend, axis=-1, keepdims=True)
    d_scores = (attend * (d_attend - inner)).astype(BF16)
    d_value_band = jnp.einsum("bhqk,bqhe->bkhe", attend_low, d_mix, preferred_element_type=F32)
    d_query = jnp.einsum("bhqk,bkhe->bqhe", d_scores, key_band, preferred_element_type=F32) * HEAD ** (-0.5)
    d_key_band = jnp.einsum("bhqk,bqhe->bkhe", d_scores, query_heads, preferred_element_type=F32) * HEAD ** (-0.5)

    def merged(band):
        parts = band.reshape(micro, count, 3 * WIN, HEADS, HEAD)
        return jnp.stack([band_back(parts[m], count) for m in range(micro)])

    stacked = jnp.stack([merged(d_key_band), merged(d_value_band)])
    stacked = stacked.reshape(2, micro, block_len + 2 * WIN, D)
    from_below = shifted(stacked[:, :, block_len + WIN :].astype(BF16), "seq", 1).astype(F32)
    from_above = shifted(stacked[:, :, :WIN].astype(BF16), "seq", -1).astype(F32)
    middle = stacked[:, :, WIN : WIN + block_len]
    middle = middle + jnp.pad(from_below, ((0, 0), (0, 0), (0, block_len - WIN), (0, 0)))
    middle = middle + jnp.pad(from_above, ((0, 0), (0, 0), (block_len - WIN, 0), (0, 0)))
    d_key_low = middle[0].astype(BF16).reshape(rows, D)
    d_value_low = middle[1].astype(BF16).reshape(rows, D)
    d_query_low = d_query.reshape(rows, D).astype(BF16)
    g["w_query"] = weight_grad(normed, d_query_low)
    g["b_query"] = jnp.sum(d_query_low.astype(F32), axis=0)
    g["w_key"] = weight_grad(normed, d_key_low)
    g["w_value"] = weight_grad(normed, d_value_low)
    g["b_value"] = jnp.sum(d_value_low.astype(F32), axis=0)
    d_normed = input_grad(d_query_low, w_query) + input_grad(d_key_low, w_key) + input_grad(d_value_low, w_value)
    _, pullback = jax.vjp(normalize, source, v["pre_gain"], v["pre_shift"])
    d_source, g["pre_gain"], g["pre_shift"] = pullback(d_normed)
    return result.reshape(micro, rows // KER // micro, D), (d_res + d_source).reshape(chars.shape), g


VECTORS = (
    "pre_gain",
    "pre_shift",
    "b_query",
    "b_value",
    "b_output",
    "mid_gain",
    "mid_shift",
    "b_down",
    "b_conv",
    "out_gain",
    "out_shift",
)
MATRICES = ("w_query", "w_key", "w_value", "w_output", "w_up", "w_down", "w_conv")
PARAMS = (
    "pre_gain",
    "pre_shift",
    "w_query",
    "b_query",
    "w_key",
    "w_value",
    "b_value",
    "w_output",
    "b_output",
    "mid_gain",
    "mid_shift",
    "w_up",
    "b_up",
    "w_down",
    "b_down",
    "w_conv",
    "b_conv",
    "out_gain",
    "out_shift",
)


def allowed_pairs(row_lengths, row_batch, micro, block_len):
    seq_count = lax.axis_size("seq")
    seq_place = lax.axis_index("seq")
    count = block_len // WIN
    buffer_len = block_len * seq_count
    places = seq_place * block_len + jnp.arange(block_len, dtype=jnp.int32)
    band_start = seq_place * block_len - WIN + WIN * jnp.arange(count, dtype=jnp.int32)
    key_places = band_start[:, None] + jnp.arange(3 * WIN, dtype=jnp.int32)[None, :]
    flat_keys = key_places.reshape(-1)
    outside = (flat_keys < 0) | (flat_keys >= buffer_len)
    query_blocks = places.reshape(count, WIN)
    near = jnp.abs(query_blocks[:, :, None] - key_places[:, None, :]) <= WIN
    result = []
    for step in range(micro):
        query_segs = segment_ids(row_lengths[0], row_batch[0], step, places).reshape(count, WIN)
        key_segs = segment_ids(row_lengths[0], row_batch[0], step, flat_keys)
        key_segs = jnp.where(outside, -2, key_segs).reshape(count, 3 * WIN)
        result.append(near & (query_segs[:, :, None] == key_segs[:, None, :]))
    return jnp.stack(result)


def per_device(characters, *rest):
    params = dict(zip(PARAMS, rest[: len(PARAMS)]))
    row_lengths, row_batch, cot_molecules = rest[len(PARAMS) :]
    seq, dp = lax.axis_size("seq"), lax.axis_size("dp")
    small = params["w_query"].shape[0]
    nz = dp // 4
    fast = seq == 2 and dp % 4 == 0 and nz > 1 and small % 8 == 0 and small <= 32
    allowed = allowed_pairs(row_lengths, row_batch, characters.shape[0], characters.shape[2])
    if fast:
        vec = jnp.zeros((16, 128), BF16)
        vec = vec.at[: len(VECTORS), :small].set(jnp.stack([params[n] for n in VECTORS]))
        vec = vec.at[len(VECTORS), : 4 * small].set(params["b_up"])
        w1, w2, vecs = gather_weights(nz, [params[n] for n in MATRICES], vec)
        w1 = w1.reshape(8, D, D)
        w2 = w2.reshape(2, 4 * D, D)
        vecs = vecs.reshape(seq * dp, 16, 128)
        full_vecs = {n: vecs[:, i, :small].reshape(D) for i, n in enumerate(VECTORS)}
        full_vecs["b_up"] = vecs[:, len(VECTORS), : 4 * small].reshape(4 * D)
        w_up = w1[4:].transpose(1, 0, 2).reshape(D, 4 * D)
        mats = (w1[0], w1[1], w1[2], w1[3], w_up, w2[0], w2[1])
    else:
        full = {n: lax.all_gather(params[n], AXES, axis=0, tiled=True) for n in PARAMS}
        mats = tuple(full[n] for n in MATRICES)
        full_vecs = {n: full[n] for n in VECTORS + ("b_up",)}
    result, grad_chars, g = layer(mats, full_vecs, characters[:, 0], cot_molecules[:, 0], allowed)
    if fast:
        g1 = jnp.concatenate(
            [
                jnp.stack([g[n].astype(BF16) for n in MATRICES[:4]]),
                g["w_up"].astype(BF16).reshape(D, 4, D).transpose(1, 0, 2),
            ]
        ).reshape(4, 2, 2, nz, 2, 2 * small, D)
        g2 = jnp.stack([g["w_down"].astype(BF16), g["w_conv"].astype(BF16)])
        g2 = g2.reshape(2, 2, nz, 2, 2, 2, 2 * small, D)
        gv = jnp.zeros((seq * dp, 16, 128), F32)
        stacked = jnp.stack([g[n] for n in VECTORS]).reshape(len(VECTORS), seq * dp, small)
        gv = gv.at[:, : len(VECTORS), :small].set(stacked.transpose(1, 0, 2))
        gv = gv.at[:, len(VECTORS), : 4 * small].set(g["b_up"].reshape(seq * dp, 4 * small))
        gv = gv.reshape(2, nz, 2, 2, 16, 128)
        out1, out2, outv = scatter_grads(nz, 2 * small, g1, g2, gv)
        out1 = out1.reshape(8, small, D)
        out2 = out2.reshape(2, 4 * small, D)
        done = {n: out1[i] for i, n in enumerate(MATRICES[:4])}
        done["w_up"] = out1[4:].transpose(1, 0, 2).reshape(small, 4 * D)
        done["w_down"], done["w_conv"] = out2[0], out2[1]
        done.update({n: outv[i, :small] for i, n in enumerate(VECTORS)})
        done["b_up"] = outv[len(VECTORS), : 4 * small]
    else:
        done = {n: lax.psum_scatter(g[n], AXES, scatter_dimension=0, tiled=True) for n in PARAMS}
    return (result[:, None], grad_chars[:, None]) + tuple(done[n] for n in PARAMS)


def solution(mesh):
    both = P(AXES)
    rows = P(AXES, None)
    acts = P(None, "dp", "seq", None)
    param_specs = tuple(rows if n in MATRICES else both for n in PARAMS)
    in_specs = (acts,) + param_specs + (P("dp", None), P("dp", None), acts)
    out_specs = (acts, acts) + param_specs
    return jax.shard_map(per_device, mesh=mesh, in_specs=in_specs, out_specs=out_specs, check_vma=False)
```

time: 1400 us -> 617 us (0.44)
  waiting for transfers between devices: 923 us -> 4.52 us
  Pallas kernels: 0 us -> 220 us
  blocking collectives: 83.6 us -> 0 us
  other arithmetic: 50.4 us -> 97 us
  matrix products: 205 us -> 172 us
  local copies, waits for them, and re-layouts: 86.6 us -> 103 us
  between operations: 16.8 us -> 2.36 us
    reduce_scatter x7 -> x0, waiting for transfers between devices: 660 us -> none  [per_device(): lax.psum_scatter(totals, ('seq', 'dp'), scatter_dimension=0, tiled=True)]
    all_gather x7 -> x0, waiting for transfers between devices: 246 us -> none  [the longest x1 56.9 us: per_device(): lax.all_gather(shards[13], ('seq', 'dp'), axis=0, tiled=True)]
    pallas_call x0 -> x2, Pallas kernels: none -> 220 us  [the longest x1 110 us: scatter_grads(): pl.pallas_call(functools.partial(scatter_kernel, nz), out_shape=(jax.Shap...]
    unnamed x2 -> x0, blocking collectives: 83.6 us -> none
    sub x0 -> x1, other arithmetic: none -> 23.4 us  [layer(): powers = jnp.exp(scores - largest)]
    another operation x3 -> x5, other arithmetic: 3.87 us -> 24.5 us  [the longest x1 3.05 us: per_device(): grad_chars = jnp.stack(grad_list)[:, None]]
    dot_general x14 -> x7, matrix products: 53.4 us -> 35.8 us  [weight_grad(): lax.dot_general(left, right, (((0,), (0,)), ((), ())), preferred_element_...]
    dot_general x26 -> x13, matrix products: 106 us -> 93.3 us  [the longest x7 37.3 us: forward_dot(): return jnp.dot(left, right, preferred_element_type=F32)]
  transfers between devices with their start and end apart: 22 -> 4, of which waited for: 15 -> 2; matrix products, arithmetic and copies ran while one was open for 16% -> 9% of each run, Pallas kernels for 0% -> 0%
where the time goes in v1:
time: 617 us; the launch traced here: 610 us
  Pallas kernels  220 us (36%)
  matrix products  172 us (28%)
  local copies, waits for them, and re-layouts  103 us (17%)
  other arithmetic  97 us (16%)
  starting transfers between devices  11.5 us (2%)
    pallas_call x1, Pallas kernels, scatter_grads(): pl.pallas_call(functools.partial(scatter_kernel, nz), out_shape=(jax.Shap...  110 us
    pallas_call x1, Pallas kernels, gather_weights(): pl.pallas_call(functools.partial(gather_kernel, nz), out_shape=(jax.Shape...  110 us
    dot_general x7, matrix products, input_grad(): lax.dot_general(left, weight, (((1,), (1,)), ((), ())), preferred_element...  42.5 us
    dot_general x7, matrix products, forward_dot(): return jnp.dot(left, right, preferred_element_type=F32)  37.3 us
    dot_general x7, matrix products, weight_grad(): lax.dot_general(left, right, (((0,), (0,)), ((), ())), preferred_element_...  35.8 us
    sub x1, other arithmetic, layer(): powers = jnp.exp(scores - largest)  23.4 us
    unnamed x187, local copies, waits for them, and re-layouts  21.1 us
    dot_general x1, matrix products, layer(): jnp.einsum('bqhe,bkhe->bhqk', d_mix, value_band, preferred_element_type=F32)  13.9 us
  transfers between devices with their start and end apart: 4, of which 2 were waited for; matrix products, arithmetic and copies ran while one was open for 9% of the time, Pallas kernels for 0%

profile of v1, /device:TPU:0, one launch (start us, length us, event | category | flops | bytes accessed | tf_op | source)
XLA Modules:
  0.0 609.5 jit_solution(17706237682189965134)
XLA Ops:
  5.2 109.8 %gather_weights.1 = (bf16[4,2,2,4,2,48,768]{6,5,4,3,2,1,0:T(8,128)(2,1)S(1)}, bf16[2,2,4,2,2,2,48,768]{7,6,5,4,3,2,1,0:T(8,128)(2,1)S(1)}, bf16[2,4,2,2,16,128]{5,4,3,2,1,0:T(8,128)(2,1)S(1)}) custom-call(bf16[24,768]{1,0:T(8,128)(2,1)S(1)} %copy-done.5, bf16[24,768]{1,0:T(8,128)(2,1)S(1)} %copy-done.6, bf16[24,768]{1,0:T(8,128)(2,1)S(1)} %copy-done.7, ...), custom_call_target="tpu_custom_call" | custom-call | tf_op jit(solution)/shard_map/gather_weights/pallas_call | solution.py:219
  136.5 4.9 slice.429
  158.2 7.2 %copy.94 = bf16[4,768,768]{1,2,0:T(8,128)(2,1)} copy(bf16[4,768,768]{2,1,0:T(8,128)(2,1)} %bitcast.401) | data formatting | bytes 9437184 | tf_op jit(solution)/shard_map/slice | solution.py:669
  167.3 8.5 %fusion.134 = (bf16[1,2,4,2,2,2,48,768]{7,6,5,4,3,2,1,0:T(8,128)(2,1)}, bf16[1,2,4,2,2,2,48,768]{7,6,5,4,3,2,1,0:T(8,128)(2,1)}) fusion(bf16[2,2,4,2,2,2,48,768]{7,6,5,4,3,2,1,0:T(8,128)(2,1)} %copy-done), kind=kLoop, calls=%fused_computation.291 | loop fusion | bytes 18874368 | tf_op jit(solution)/shard_map/slice | solution.py:670
  179.7 6.7 %copy.86 = bf16[2,2,768,768]{2,3,1,0:T(8,128)(2,1)} copy(bf16[2,2,768,768]{3,2,1,0:T(8,128)(2,1)} %pad_maximum_fusion.1) | data formatting | bytes 9437184 | tf_op jit(solution)/shard_map/concatenate | solution.py:495
  191.3 8.4 %fusion.81 = f32[8,12,128,384]{3,2,1,0:T(8,128)} fusion(bf16[8,384,12,64]{1,3,2,0:T(8,128)(2,1)S(1)} %get-tuple-element.185, bf16[8,128,12,64]{1,0,3,2:T(8,128)(2,1)S(1)} %bitcast.406), kind=kOutput, calls=%fused_computation.108 | convolution fusion | flops 603979776 | bytes 25165824 | tf_op jit(solution)/shard_map/bqhe,bkhe->bhqk/dot_general | solution.py:515
  200.8 23.4 %fusion.139 = (f32[8,12,128]{2,1,0:T(8,128)S(1)}, f32[8,12,128,384]{3,2,1,0:T(8,128)}) fusion(f32[8,12,128,384]{3,2,1,0:T(8,128)} %fusion.81, pred[8,128,384]{2,1,0:T(8,128)(4,1)} %bitcast.451), kind=kOutput, calls=%fused_computation.296 | output fusion | flops 28311936 | bytes 38191104 | tf_op jit(solution)/shard_map/sub | solution.py:519
  224.9 10.2 %fusion.53 = bf16[8,128,12,64]{1,3,2,0:T(8,128)(2,1)S(1)} fusion(bf16[8,384,12,64]{1,3,2,0:T(8,128)(2,1)} %copy-done.42, f32[8,12,128,384]{3,2,1,0:T(8,128)} %get-tuple-element.250, f32[8,12,128]{2,1,0:T(8,128)S(1)} %get-tuple-element.249), kind=kOutput, calls=%fused_computation.90 | convolution fusion | flops 614203392 | bytes 25214976 | tf_op jit(solution)/shard_map/bhqk,bkhe->bqhe/dot_general | solution.py:523
  240.6 8.2 %fusion.127 = f32[1024,3072]{1,0:T(8,128)} fusion(bf16[768,3072]{0,1:T(8,128)(2,1)S(1)} %bitcast.427, f32[1024,768]{1,0:T(8,128)S(1)} %get-tuple-element.252, f32[768]{0:T(1024)S(1)} %copy-done.56, f32[768]{0:T(1024)S(1)} %reshape.887, f32[1024]{0:T(1024)S(1)} %fusion.116, f32[1024]{0:T(1024)S(1)} %broadcast_multiply_fusion), kind=kOutput, calls=%fused_computation.285 | convolution fusion | flops 4835770368 | bytes 20461568 | tf_op jit(solution)/shard_map/dot_general | solution.py:42
  248.8 10.7 %add_convert_fusion = bf16[1024,768]{1,0:T(8,128)(2,1)S(1)} fusion(f32[1024,768]{1,0:T(8,128)S(1)} %get-tuple-element.252, bf16[3072,768]{1,0:T(8,128)(2,1)S(1)} %bitcast.432, f32[768]{0:T(1024)S(1)} %copy-done.60, f32[1024,3072]{1,0:T(8,128)} %fusion.127, f32[3072]{0:T(1024)S(1)} %copy-done.53), kind=kOutput, calls=%fused_computation.65 | convolution fusion | flops 4865654784 | bytes 22035456 | tf_op jit(solution)/shard_map/dot_general | solution.py:42
  273.7 17.4 %fusion.142 = (f32[3072]{0:T(1024)}, bf16[1024,3072]{1,0:T(8,128)(2,1)S(1)}) fusion(f32[1024,3072]{1,0:T(8,128)} %fusion.127, f32[3072]{0:T(1024)S(1)} %copy-done.54, bf16[1024,768]{1,0:T(8,128)(2,1)} %convert_element_type.341, bf16[3072,768]{1,0:T(8,128)(2,1)} %bitcast.429), kind=kOutput, calls=%fused_computation.299 | convolution fusion | flops 4901041152 | bytes 25190400 | tf_op jit(solution)/shard_map/dot_general | solution.py:50
  291.1 8.5 %multiply_reduce_fusion.1 = (f32[768]{0:T(1024)}, f32[1024]{0:T(1024)S(1)}, f32[768]{0:T(1024)}, f32[1024,768]{1,0:T(8,128)S(1)}) fusion(f32[1024,768]{1,0:T(8,128)S(1)} %copy-done.24, f32[1024]{0:T(1024)S(1)} %copy-done.51, f32[1024]{0:T(1024)S(1)} %broadcast_multiply_fusion, f32[768]{0:T(1024)S(1)} %reshape.887, bf16[768,3072]{0,1:T(8,128)(2,1)} %bitcast.424, ...), kind=kOutput, calls=%fused_computation.54 | convolution fusion | flops 4838126592 | bytes 17323008 | tf_op jit(solution)/shard_map/dot_general | solution.py:50
  299.7 7.8 %convolution_convert_fusion.1 = bf16[768,3072]{1,0:T(8,128)(2,1)} fusion(bf16[1024,3072]{1,0:T(8,128)(2,1)S(1)} %get-tuple-element.264, f32[1024,768]{1,0:T(8,128)S(1)} %copy-done.24, f32[768]{0:T(1024)S(1)} %copy-done.57, f32[768]{0:T(1024)S(1)} %reshape.887, f32[1024]{0:T(1024)S(1)} %copy-done.51, f32[1024]{0:T(1024)S(1)} %broadcast_multiply_fusion), kind=kOutput, calls=%fused_computation.26 | convolution fusion | flops 4838129664 | bytes 14170112 | tf_op jit(solution)/shard_map/dot_general | solution.py:46
  316.6 12.6 %convolution_convert_fusion = bf16[3072,768]{1,0:T(8,128)(2,1)} fusion(f32[1024,768]{1,0:T(8,128)S(1)} %reshape.873, f32[1024,3072]{1,0:T(8,128)} %fusion.127, f32[3072]{0:T(1024)S(1)} %copy-done.54), kind=kOutput, calls=%fused_computation.25 | convolution fusion | flops 4866441216 | bytes 20459520 | tf_op jit(solution)/shard_map/dot_general | solution.py:46
  335.3 11.1 %fusion.18 = f32[8,384,12,64]{1,3,2,0:T(8,128)} fusion(bf16[8,128,12,64]{1,0,3,2:T(8,128)(2,1)S(1)} %bitcast.444, f32[8,12,128,384]{3,2,1,0:T(8,128)} %get-tuple-element.250, f32[8,12,128]{2,1,0:T(8,128)S(1)} %copy-done.45), kind=kOutput, calls=%fused_computation.37 | convolution fusion | flops 613416960 | bytes 29933568 | tf_op jit(solution)/shard_map/bhqk,bqhe->bkhe/dot_general | solution.py:564
  346.4 13.9 %multiply_reduce_fusion = (f32[8,12,128]{2,1,0:T(8,128)S(1)}, f32[8,12,128,384]{3,2,1,0:T(8,128)}) fusion(f32[8,12,128,384]{3,2,1,0:T(8,128)} %get-tuple-element.250, f32[8,12,128]{2,1,0:T(8,128)S(1)} %copy-done.45, bf16[8,384,12,64]{1,3,2,0:T(8,128)(2,1)} %copy-done.42, bf16[8,128,12,64]{1,0,3,2:T(8,128)(2,1)S(1)} %bitcast.445), kind=kOutput, calls=%fused_computation.2 | convolution fusion | flops 618123264 | bytes 44138496 | tf_op jit(solution)/shard_map/bqhe,bkhe->bhqk/dot_general | solution.py:561
  360.3 13.3 %multiply_convert_fusion = bf16[8,12,128,384]{3,2,1,0:T(8,128)(2,1)S(1)} fusion(f32[8,12,128,384]{3,2,1,0:T(8,128)} %get-tuple-element.259, f32[8,12,128]{2,1,0:T(8,128)S(1)} %get-tuple-element.258, f32[8,12,128,384]{3,2,1,0:T(8,128)} %get-tuple-element.250, f32[8,12,128]{2,1,0:T(8,128)S(1)} %copy-done.45), kind=kLoop, calls=%fused_computation.1 | loop fusion | flops 18874368 | bytes 47284224 | tf_op jit(solution)/shard_map/convert_element_type | solution.py:563
  373.6 7.9 %convert_reduce_fusion.2 = (f32[12,64]{1,0:T(8,128)S(1)}, bf16[8,128,12,64]{1,3,2,0:T(8,128)(2,1)}) fusion(bf16[8,384,12,64]{1,3,2,0:T(8,128)(2,1)} %copy-done.14, bf16[8,12,128,384]{3,2,1,0:T(8,128)(2,1)S(1)} %multiply_convert_fusion), kind=kOutput, calls=%fused_computation.56 | convolution fusion | flops 607124736 | bytes 15731712 | tf_op jit(solution)/shard_map/bhqk,bkhe->bqhe/dot_general | solution.py:565
  386.1 5.9 slice_bitcast_fusion.7
  402.4 5.9 slice_bitcast_fusion.15
  419.8 7.1 %fusion.128 = bf16[2,2,768,768]{3,2,1,0:T(8,128)(2,1)} fusion(f32[1,1,768,768]{3,2,1,0:T(8,128)} %copy.107, f32[1,1,768,768]{3,2,1,0:T(8,128)S(1)} %copy.106, f32[1,1,768,768]{3,2,1,0:T(8,128)} %copy.104, f32[1,1,768,768]{3,2,1,0:T(8,128)} %copy.103), kind=kLoop, calls=%fused_computation.286 | loop fusion | flops 7077888 | bytes 14155776 | tf_op jit(solution)/shard_map/convert.21
  436.0 5.4 collective-permute-start.2
  449.6 8.3 %pad_maximum_fusion.g2 = bf16[2,2,4,2,2,2,48,768]{7,6,5,4,3,2,1,0:T(8,128)(2,1)} fusion(bf16[1,2,4,2,2,2,48,768]{7,6,5,4,3,2,1,0:T(8,128)(2,1)} %bitcast.400, bf16[1,2,4,2,2,2,48,768]{7,6,5,4,3,2,1,0:T(8,128)(2,1)} %bitcast.428), kind=kLoop, calls=%fused_computation.16 | loop fusion | flops 4718592 | bytes 18874368 | tf_op jit(solution)/shard_map/stack | solution.py:683
  490.5 109.8 %scatter_grads.1 = (f32[4,2,24,768]{3,2,1,0:T(8,128)}, f32[2,2,48,768]{3,2,1,0:T(8,128)}, f32[16,128]{1,0:T(8,128)}) custom-call(bf16[4,2,2,4,2,48,768]{6,5,4,3,2,1,0:T(8,128)(2,1)} %bitcast.412, bf16[2,2,4,2,2,2,48,768]{7,6,5,4,3,2,1,0:T(8,128)(2,1)} %pad_maximum_fusion.g2, f32[2,4,2,2,16,128]{5,4,3,2,1,0:T(8,128)} %bitcast.449), custom_call_target="tpu_custom_call" | custom-call | tf_op jit(solution)/shard_map/scatter_grads/pallas_call | solution.py:438
  (324 shorter events, 174.3 us)
Async XLA Ops:
  0.7 122.1 %copy-start.9 = (bf16[2,1,512,768]{3,2,1,0:T(8,128)(2,1)S(1)}, bf16[2,1,512,768]{3,2,1,0:T(8,128)(2,1)}, u32[]{:S(2)}) copy-start(bf16[2,1,512,768]{3,2,1,0:T(8,128)(2,1)} %param.31) | copy-start | bytes 4718596
  131.6 44.2 %collective-permute-start = (bf16[2,2,128,768]{3,2,1,0:T(8,128)(2,1)}, bf16[2,2,128,768]{3,2,1,0:T(8,128)(2,1)}, u32[]{:S(2)}, u32[]{:S(2)}) collective-permute-start(bf16[2,2,128,768]{3,2,1,0:T(8,128)(2,1)} %get-tuple-element.204), channel_id=1, source_target_pairs={{0,16},{1,17},{2,18},{3,19},{4,20},{5,21},{6,22},{7,23},{8,24},{9,... | collective-permute-start | bytes 2359304 | tf_op jit(solution)/shard_map/ppermute | solution.py:488
  135.1 40.6 %collective-permute-start.1 = (bf16[2,2,128,768]{3,2,1,0:T(8,128)(2,1)}, bf16[2,2,128,768]{3,2,1,0:T(8,128)(2,1)}, u32[]{:S(2)}, u32[]{:S(2)}) collective-permute-start(bf16[2,2,128,768]{3,2,1,0:T(8,128)(2,1)} %get-tuple-element.205), channel_id=1, source_target_pairs={{16,0},{17,1},{18,2},{19,3},{20,4},{21,5},{22,6},{23,7},{24,8},{25... | collective-permute-start | bytes 2359304 | tf_op jit(solution)/shard_map/ppermute | solution.py:488
  158.2 33.1 %copy-start.18 = (bf16[96,8,8,128]{3,2,1,0:T(8,128)(2,1)}, bf16[96,8,8,128]{3,2,1,0:T(8,128)(2,1)S(1)}, u32[]{:S(2)}) copy-start(bf16[96,8,8,128]{3,2,1,0:T(8,128)(2,1)S(1)} %copy.126) | copy-start | bytes 4718596
  167.3 8.5 %copy-start.26 = (bf16[1024,768]{1,0:T(8,128)(2,1)S(1)}, bf16[1024,768]{1,0:T(8,128)(2,1)}, u32[]{:S(2)}) copy-start(bf16[1024,768]{1,0:T(8,128)(2,1)} %copy-done.25) | copy-start | bytes 4718596
  167.3 8.5 %copy-start.28 = (bf16[1024,768]{1,0:T(8,128)(2,1)S(1)}, bf16[1024,768]{1,0:T(8,128)(2,1)}, u32[]{:S(2)}) copy-start(bf16[1024,768]{1,0:T(8,128)(2,1)} %copy-done.27) | copy-start | bytes 4718596
  191.3 8.4 %copy-start.14 = (bf16[8,384,12,64]{1,3,2,0:T(8,128)(2,1)}, bf16[8,384,12,64]{1,3,2,0:T(8,128)(2,1)S(1)}, u32[]{:S(2)}) copy-start(bf16[8,384,12,64]{1,3,2,0:T(8,128)(2,1)S(1)} %get-tuple-element.185) | copy-start | bytes 14155780
  191.3 9.6 %copy-start.42 = (bf16[8,384,12,64]{1,3,2,0:T(8,128)(2,1)}, bf16[8,384,12,64]{1,3,2,0:T(8,128)(2,1)S(1)}, u32[]{:S(2)}) copy-start(bf16[8,384,12,64]{1,3,2,0:T(8,128)(2,1)S(1)} %get-tuple-element.186) | copy-start | bytes 14155780
  239.9 8.9 %copy-start.23 = (f32[1024,768]{1,0:T(8,128)}, f32[1024,768]{1,0:T(8,128)S(1)}, u32[]{:S(2)}) copy-start(f32[1024,768]{1,0:T(8,128)S(1)} %get-tuple-element.252) | copy-start | bytes 9437188
  239.9 8.8 %slice-start.6 = ((s8[4718592]{0:T(1024)(128)(4,1)}), s8[4194304]{0:T(1024)(128)(4,1)S(1)}, s32[]{:S(2)}) async-start(s8[4718592]{0:T(1024)(128)(4,1)} %bitcast.430), calls=%async_computation.6 | async-start | bytes 8388608
  240.4 8.3 %copy-start.50 = (f32[1024]{0:T(1024)}, f32[1024]{0:T(1024)S(1)}, u32[]{:S(2)}) copy-start(f32[1024]{0:T(1024)S(1)} %fusion.116) | copy-start | bytes 12292
  240.6 8.2 %slice-start.7 = ((s8[4718592]{0:T(1024)(128)(4,1)}), s8[524288]{0:T(1024)(128)(4,1)S(1)}, s32[]{:S(2)}) async-start(s8[4718592]{0:T(1024)(128)(4,1)} %bitcast.430), calls=%async_computation.7 | async-start | bytes 1048576
  240.6 8.2 %copy-start.53 = (f32[3072]{0:T(1024)S(1)}, f32[3072]{0:T(1024)}, u32[]{:S(2)}) copy-start(f32[3072]{0:T(1024)} %reshape.889) | copy-start | bytes 36868
  240.6 8.2 %copy-start.60 = (f32[768]{0:T(1024)S(1)}, f32[768]{0:T(1024)}, u32[]{:S(2)}) copy-start(f32[768]{0:T(1024)} %reshape.890) | copy-start | bytes 9220
  260.7 8.1 %slice-start = ((s8[4718592]{0:T(1024)(128)(4,1)}), s8[4194304]{0:T(1024)(128)(4,1)S(1)}, s32[]{:S(2)}) async-start(s8[4718592]{0:T(1024)(128)(4,1)} %bitcast.403), calls=%async_computation | async-start | bytes 8388608
  260.7 8.1 %slice-start.1 = ((s8[4718592]{0:T(1024)(128)(4,1)}), s8[524288]{0:T(1024)(128)(4,1)S(1)}, s32[]{:S(2)}) async-start(s8[4718592]{0:T(1024)(128)(4,1)} %bitcast.403), calls=%async_computation.1 | async-start | bytes 1048576
  273.7 17.4 %copy-start.24 = (f32[1024,768]{1,0:T(8,128)S(1)}, f32[1024,768]{1,0:T(8,128)}, u32[]{:S(2)}) copy-start(f32[1024,768]{1,0:T(8,128)} %copy-done.23) | copy-start | bytes 9437188
  273.7 17.4 %copy-start.51 = (f32[1024]{0:T(1024)S(1)}, f32[1024]{0:T(1024)}, u32[]{:S(2)}) copy-start(f32[1024]{0:T(1024)} %copy-done.50) | copy-start | bytes 12292
  291.1 8.5 %copy-start.57 = (f32[768]{0:T(1024)S(1)}, f32[768]{0:T(1024)}, u32[]{:S(2)}) copy-start(f32[768]{0:T(1024)} %reshape.888) | copy-start | bytes 9220
  316.6 12.6 %copy-start.22 = (f32[1024,768]{1,0:T(8,128)S(1)}, f32[1024,768]{1,0:T(8,128)}, u32[]{:S(2)}) copy-start(f32[1024,768]{1,0:T(8,128)} %get-tuple-element.164) | copy-start | bytes 9437188
  431.7 11.0 %copy-start.34 = (bf16[2,1,512,768]{3,2,1,0:T(8,128)(2,1)S(1)}, bf16[2,1,512,768]{3,2,1,0:T(8,128)(2,1)}, u32[]{:S(2)}) copy-start(bf16[2,1,512,768]{3,2,1,0:T(8,128)(2,1)} %copy-done.33) | copy-start | bytes 4718596
  436.0 22.2 %collective-permute-start.2 = (bf16[2,2,128,768]{3,2,1,0:T(8,128)(2,1)S(1)}, bf16[2,2,128,768]{3,2,1,0:T(8,128)(2,1)S(1)}, u32[]{:S(2)}, u32[]{:S(2)}) collective-permute-start(bf16[2,2,128,768]{3,2,1,0:T(8,128)(2,1)S(1)} %get-tuple-element.183), channel_id=1, source_target_pairs={{0,16},{1,17},{2,18},{3,19},{4,20},{5,21},{6,22},{7,23},{8,24},{9,... | collective-permute-start | bytes 2359304 | tf_op jit(solution)/shard_map/ppermute | solution.py:488
  441.4 20.9 %collective-permute-start.3 = (bf16[2,2,128,768]{3,2,1,0:T(8,128)(2,1)S(1)}, bf16[2,2,128,768]{3,2,1,0:T(8,128)(2,1)S(1)}, u32[]{:S(2)}, u32[]{:S(2)}) collective-permute-start(bf16[2,2,128,768]{3,2,1,0:T(8,128)(2,1)S(1)} %get-tuple-element.184), channel_id=1, source_target_pairs={{16,0},{17,1},{18,2},{19,3},{20,4},{21,5},{22,6},{23,7},{24,8},{25... | collective-permute-start | bytes 2359304 | tf_op jit(solution)/shard_map/ppermute | solution.py:488
  490.5 112.6 %copy-start.13 = (f32[1024,768]{1,0:T(8,128)S(1)}, f32[1024,768]{1,0:T(8,128)}, u32[]{:S(2)}) copy-start(f32[1024,768]{1,0:T(8,128)} %copy-done.12) | copy-start | bytes 9437188
  (63 other events, 255.1 us)

commit v2 on v1

v2 whole, which is shorter than its diff:
```python
import functools
import typing

import jax
import jax.numpy as jnp
from jax import lax
from jax.experimental import pallas as pl
from jax.experimental.pallas import tpu as pltpu
from jax.sharding import PartitionSpec as P

D = 768
HEADS = 12
HEAD = 64
KER = 4
WIN = 128
EPSILON = 1e-05
MESH = pl.DeviceIdType.MESH
AXES = ("seq", "dp")
F32 = jnp.float32
BF16 = jnp.bfloat16


def normalize(vector, gain, shift):
    average = jnp.mean(vector, axis=-1, keepdims=True)
    centered = vector - average
    variance = jnp.mean(centered * centered, axis=-1, keepdims=True)
    return centered * lax.rsqrt(variance + EPSILON) * gain + shift


def segment_ids(lengths, batches, micro_step, places):
    slot_ids = jnp.arange(lengths.shape[0], dtype=jnp.int32)
    before = (slot_ids[:, None] < slot_ids[None, :]) & (batches[:, None] == batches[None, :])
    starts = jnp.sum(jnp.where(before, lengths[:, None], 0), axis=0)
    inside = (
        (batches[:, None] == micro_step)
        & (places[None, :] >= starts[:, None])
        & (places[None, :] < (starts + lengths)[:, None])
    )
    return jnp.sum(jnp.where(inside, slot_ids[:, None] + 1, 0), axis=0) - 1


def forward_dot(left, right):
    return jnp.dot(left, right, preferred_element_type=F32)


def weight_grad(left, right):
    return lax.dot_general(left, right, (((0,), (0,)), ((), ())), preferred_element_type=F32)


def input_grad(left, weight):
    return lax.dot_general(left, weight, (((1,), (1,)), ((), ())), preferred_element_type=F32)


class Place:
    def __init__(self, nz):
        self.nz = nz
        dp = lax.axis_index("dp")
        self.x = lax.axis_index("seq")
        self.core = lax.rem(dp, 2)
        self.y = lax.rem(dp // 2, 2)
        self.z = dp // 4

    def device(self, x=None, z=None, y=None, core=None):
        x = self.x if x is None else x
        z = self.z if z is None else z
        y = self.y if y is None else y
        core = self.core if core is None else core
        return (x, z * 4 + y * 2 + core)

    def partner(self):
        return self.device(core=1 - self.core)

    def across_x(self):
        return self.device(x=1 - self.x)

    def across_y(self):
        return self.device(y=1 - self.y)

    def z_ahead(self, offset):
        return lax.rem(self.z + offset, self.nz)

    def along_z(self, offset):
        return self.device(z=self.z_ahead(offset))


def greet(place):
    barrier = pltpu.get_barrier_semaphore()
    others = [place.partner(), place.across_x(), place.across_y()]
    others += [place.along_z(o) for o in range(1, place.nz)]
    for other in others:
        pl.semaphore_signal(barrier, inc=1, device_id=other, device_id_type=MESH)
    pl.semaphore_wait(barrier, len(others))


class Sender:
    def __init__(self, send_sems, recv_sems):
        self.send_sems, self.recv_sems = send_sems, recv_sems
        self.count = 0
        self.open = []

    def hold(self, src, dst, device):
        number = self.count
        self.count += 1

        def copy():
            return pltpu.make_async_remote_copy(
                src_ref=src(),
                dst_ref=dst(),
                send_sem=self.send_sems.at[number],
                recv_sem=self.recv_sems.at[number],
                device_id=device(),
                device_id_type=MESH,
            )

        return copy

    def start(self, src, dst, device):
        copy = self.hold(src, dst, device)
        copy().start()
        self.open.append(copy)
        return copy

    def finish(self):
        for copy in self.open:
            copy().wait_send()


UNITS = 8
PARTS = (
    (pl.ds(0, 256), ("z", "x", "y")),
    (pl.ds(256, 256), ("z", "y", "x")),
    (pl.ds(512, 128), ("y", "z", "x")),
    (pl.ds(640, 128), ("x", "z", "y")),
)


AHEAD = 1
LAGS = (1, 2, 3, 4)


class Grid:
    def __init__(self, nz):
        self.place = Place(nz)
        self.size = {"x": 2, "z": nz, "y": 2}
        self.here = {"x": self.place.x, "z": self.place.z, "y": self.place.y}

    def peers(self, axis):
        place = self.place
        if axis == "x":
            return [(place.across_x, lambda: 1 - place.x)]
        if axis == "y":
            return [(place.across_y, lambda: 1 - place.y)]
        steps = range(1, self.size["z"])
        return [(functools.partial(place.along_z, o), functools.partial(place.z_ahead, o)) for o in steps]

    def index(self, full, given=()):
        given = dict(given)
        return tuple(given.get(a, slice(None) if a in full else self.here[a]) for a in ("x", "z", "y"))


def cut(ref, unit, core, index, columns=None):
    columns = slice(None) if columns is None else columns
    if unit < 4:
        return ref[0].at[(unit, core) + index + (slice(None), columns)]
    return ref[1].at[((unit - 4) // 2,) + index + (core, unit % 2, slice(None), columns)]


class Gather:
    def __init__(self, grid, sender, ref, vecs):
        self.grid, self.sender, self.ref, self.vecs = grid, sender, ref, vecs
        self.core = grid.place.core
        self.going = {}
        self.vgoing = []
        self.rounds = 0

    def launch(self, unit, part, phase):
        columns, order = PARTS[part]
        done, axis = order[:phase], order[phase]

        def block():
            return cut(self.ref, unit, self.core, self.grid.index(done), columns)

        self.going[unit, part] = [self.sender.start(block, block, device) for device, _ in self.grid.peers(axis)]

    def launch_core(self, unit):
        def block():
            return cut(self.ref, unit, self.core, (slice(None),) * 3)

        self.going[unit, 0] = [self.sender.start(block, block, self.grid.place.partner)]

    def arrived(self, unit, part):
        for copy in self.going.pop((unit, part)):
            copy().wait_recv()

    def vec_step(self, phase):
        for copy in self.vgoing:
            copy().wait_recv()
        self.vgoing = []
        if phase < 3:
            order = ("z", "y", "x")

            def block():
                return self.vecs.at[self.grid.index(order[:phase])]

            self.vgoing = [self.sender.start(block, block, d) for d, _ in self.grid.peers(order[phase])]

    def round(self):
        r = self.rounds
        self.rounds += 1
        if r < 4:
            self.vec_step(r)
        for unit in range(AHEAD + 1) if r == 0 else (r + AHEAD,):
            if unit < UNITS:
                for part in range(len(PARTS)):
                    self.launch(unit, part, 0)
        for phase in (1, 2):
            unit = r - LAGS[phase - 1]
            if 0 <= unit < UNITS:
                for part in range(len(PARTS)):
                    self.arrived(unit, part)
                    self.launch(unit, part, phase)
        unit = r - LAGS[2]
        if 0 <= unit < UNITS:
            for part in range(len(PARTS)):
                self.arrived(unit, part)
            self.launch_core(unit)
        unit = r - LAGS[3]
        if 0 <= unit < UNITS:
            self.arrived(unit, 0)


def gather_copies(nz):
    return UNITS * (len(PARTS) * (nz + 1) + 1) + nz + 1


def loop(count, body, hooks=None):
    hooks = hooks or {}

    def step(i, carry):
        body(i)
        for at, hook in hooks.items():
            pl.when(i == at)(lambda hook=hook: hook())
        return carry

    lax.fori_loop(0, count, step, 0)


def staged(count, slots, dst, sem, body, hooks=None):
    def copy(i):
        slot = lax.rem(i, 2)
        return pltpu.make_async_copy(slots.at[slot], dst(i), sem.at[slot])

    def step(i):
        @pl.when(i >= 2)
        def _():
            copy(i - 2).wait()

        body(i, lax.rem(i, 2))
        copy(i).start()

    loop(count, step, hooks)

    def end():
        for i in range(max(0, count - 2), count):
            copy(i).wait()

    return end


def dot(a, b):
    return jnp.dot(a, b, preferred_element_type=F32)


def dot_t(a, b):
    return lax.dot_general(a, b, (((1,), (1,)), ((), ())), preferred_element_type=F32)


def spread_vectors(nz, small, vecs, vfull, vup):
    group = 384 // small
    lane = lax.broadcasted_iota(jnp.int32, (group * 128, 384), 1)
    row = lax.broadcasted_iota(jnp.int32, (group * 128, 384), 0)
    field = lax.rem(row, 128)
    place = (lane == row // 128 * small + field) & (field < small)
    pick = jnp.where(place, 1.0, 0.0).astype(BF16)
    tiles = [vecs[d // (4 * nz), (d // 4) % nz, (d // 2) % 2, d % 2] for d in range(8 * nz)]
    for g in range(2):
        left = jnp.concatenate(tiles[g * group : (g + 1) * group], axis=1)
        vfull[:, g * 384 : (g + 1) * 384] = dot(left, pick)
    group = group // 4
    lane, row = lane[: group * 128], row[: group * 128]
    field = lax.rem(row, 128)
    place = (lane == row // 128 * (4 * small) + field) & (field < 4 * small)
    pick = jnp.where(place, 1.0, 0.0).astype(BF16)
    for g in range(8):
        left = jnp.concatenate(tiles[g * group : (g + 1) * group], axis=1)
        line = dot(left, pick)[len(VECTORS) : len(VECTORS) + 1]
        vup[g // 2, :, (g % 2) * 384 : (g % 2 + 1) * 384] = jnp.broadcast_to(line, (8, 384))


def crossing(lens, bats, micro, edge):
    start = jnp.int32(0)
    below, above = jnp.int32(-1), jnp.int32(-1)
    for s in range(lens.shape[1]):
        length = jnp.where(bats[0, s] == micro, lens[0, s], 0)
        end = start + length
        below = jnp.where((start <= edge - 1) & (edge - 1 < end), s, below)
        above = jnp.where((start <= edge) & (edge < end), s, above)
        start = end
    return below == above


C0 = 0.7978845608028654
C1 = 0.044715


def gelu_parts(v):
    square = v * v
    t = jnp.tanh(C0 * v * (1.0 + C1 * square))
    half = 0.5 * (1.0 + t)
    slope = half + (0.5 * C0) * v * (1.0 - t * t) * (1.0 + (3.0 * C1) * square)
    return v * half, slope


class ForwardRefs(typing.NamedTuple):
    lens: typing.Any
    bats: typing.Any
    chars: typing.Any
    wq: typing.Any
    wk: typing.Any
    wv: typing.Any
    wo: typing.Any
    wu: typing.Any
    wd: typing.Any
    wc: typing.Any
    vec: typing.Any
    w1o: typing.Any
    w2o: typing.Any
    vfull: typing.Any
    normedT_o: typing.Any
    q_o: typing.Any
    v_o: typing.Any
    kT_o: typing.Any
    pt_o: typing.Any
    mixT_o: typing.Any
    res_o: typing.Any
    normed2T_o: typing.Any
    gp_o: typing.Any
    actT_o: typing.Any
    grp_o: typing.Any
    conv_o: typing.Any
    mol_o: typing.Any
    w1: typing.Any
    w2: typing.Any
    vecs: typing.Any
    own: typing.Any
    pre: typing.Any
    vup: typing.Any
    hchars: typing.Any
    normed: typing.Any
    q: typing.Any
    k: typing.Any
    v: typing.Any
    vT: typing.Any
    stage: typing.Any
    pstage: typing.Any
    mixT: typing.Any
    res: typing.Any
    res2: typing.Any
    normed2: typing.Any
    act: typing.Any
    gstage: typing.Any
    grp: typing.Any
    band: typing.Any
    send_sems: typing.Any
    recv_sems: typing.Any
    csem: typing.Any
    psem: typing.Any
    wsem: typing.Any
    gsem: typing.Any


class Saved(typing.NamedTuple):
    w1o: typing.Any
    w2o: typing.Any
    vfull: typing.Any
    normedT_o: typing.Any
    q_o: typing.Any
    v_o: typing.Any
    kT_o: typing.Any
    pt_o: typing.Any
    mixT_o: typing.Any
    res_o: typing.Any
    normed2T_o: typing.Any
    gp_o: typing.Any
    actT_o: typing.Any
    grp_o: typing.Any
    conv_o: typing.Any
    mol_o: typing.Any


def forward_kernel(nz, small, *refs):
    r = ForwardRefs(*refs)
    grid = Grid(nz)
    place = grid.place
    x, y, z, core = place.x, place.y, place.z, place.core
    sender = Sender(r.send_sems, r.recv_sems)
    micro, length = r.chars.shape[0], r.chars.shape[1]
    count = length // WIN
    ext = length + 2 * WIN

    for m, ref in enumerate((r.wq, r.wk, r.wv, r.wo)):
        r.own[m % 2, m // 2] = ref[...]
    for j in range(4):
        r.own[j % 2, 2 + j // 2] = r.wu[:, j * D : (j + 1) * D]
    for t in range(4):
        r.pre[core, t] = r.own[core, t]
    r.vecs[x, z, y, core] = r.vec[...]
    for p, ref in enumerate((r.wd, r.wc)):
        for half in range(2):
            r.w2[p, x, z, y, core, half] = ref[half]
    greet(place)
    swap = sender.start(lambda: r.own.at[1 - core], lambda: r.pre.at[core], place.partner)

    def mine():
        return r.vecs.at[x, z, y, core]

    vswap = sender.start(mine, mine, place.partner)

    def edge():
        return r.chars.at[:, pl.ds(pl.multiple_of((1 - x) * (length - WIN), WIN), WIN)]

    halo = sender.start(edge, lambda: r.hchars, place.across_x)
    swap().wait_recv()
    vswap().wait_recv()
    for t in range(4):
        both = [r.pre[i, t].astype(F32) for i in range(2)]
        r.w1[t, core, x, z, y] = jnp.concatenate(both, axis=0).astype(BF16)
    gather = Gather(grid, sender, (r.w1, r.w2), r.vecs)
    for _ in range(4):
        gather.round()
    spread_vectors(nz, small, r.vecs, r.vfull, r.vup)

    def vector(name):
        n = VECTORS.index(name)
        return r.vfull[n : n + 1, :]

    key = lax.broadcasted_iota(jnp.int32, (WIN, WIN), 0)
    query = lax.broadcasted_iota(jnp.int32, (WIN, WIN), 1)
    for side in range(2):
        near = key >= query if side == 0 else key <= query
        for m in range(micro):
            joined = crossing(r.lens, r.bats, m, length) & (x == 1 - side)
            r.band[side, m] = jnp.where(near, jnp.where(joined, 0.0, -1e30), -1e30)
        r.band[side, micro] = jnp.where(near, 0.0, -1e30)

    def norm_rows(i):
        m, b = i // count, lax.rem(i, count)
        rows = r.chars[m, pl.ds(pl.multiple_of(b * WIN, WIN), WIN)].astype(F32)
        out = normalize(rows, vector("pre_gain"), vector("pre_shift")).astype(BF16)
        r.normed[m, pl.ds(pl.multiple_of((b + 1) * WIN, WIN), WIN)] = out

    loop(micro * count, norm_rows)
    halo().wait_recv()
    for m in range(micro):
        out = normalize(r.hchars[m].astype(F32), vector("pre_gain"), vector("pre_shift")).astype(BF16)
        r.normed[m, pl.ds(pl.multiple_of((1 - x) * (length + WIN), WIN), WIN)] = out
        zero = jnp.zeros((WIN, D), BF16)
        r.normed[m, pl.ds(pl.multiple_of(x * (length + WIN), WIN), WIN)] = zero

    def turn(src, row, slot, lane):
        r.stage[slot, :, pl.ds(pl.multiple_of(lane * WIN, WIN), WIN)] = src[row].T

    def turn_normed(m, slot):
        for b in range(count):
            r.stage[slot, :, b * WIN : (b + 1) * WIN] = r.normed[m, (b + 1) * WIN : (b + 2) * WIN].T

    short = r.stage.at[:, :, pl.ds(0, length)]
    end = staged(micro, short, lambda m: r.normedT_o.at[m], r.csem, turn_normed)
    tile = 256
    copies = []

    def save(src, dst, n):
        copies.append(pltpu.make_async_copy(src.at[n], dst.at[n], r.wsem.at[len(copies)]))
        copies[-1].start()

    def matrix(t, c):
        return r.w1[t, c].reshape(D, D)

    gather.round()
    per = length // tile

    def make_q(i):
        m, b = i // per, lax.rem(i, per)
        rows = r.normed[m, pl.ds(pl.multiple_of(WIN + b * tile, WIN), tile)]
        out = (dot(rows, matrix(0, 0)) + vector("b_query")).astype(BF16)
        r.q[m, pl.ds(pl.multiple_of(b * tile, tile), tile)] = out * jnp.asarray(HEAD ** (-0.5), BF16)

    loop(micro * per, make_q)
    pere = ext // tile

    def make_k(i):
        m, rows = i // pere, pl.ds(pl.multiple_of(lax.rem(i, pere) * tile, tile), tile)
        r.k[m, rows] = dot(r.normed[m, rows], matrix(0, 1)).astype(BF16)

    loop(micro * pere, make_k)

    def turn_k(m, slot):
        for b in range(ext // WIN):
            r.stage[slot, :, b * WIN : (b + 1) * WIN] = r.k[m, b * WIN : (b + 1) * WIN].T

    end()
    end = staged(micro, r.stage, lambda m: r.kT_o.at[m], r.csem, turn_k)
    for m in range(micro):
        save(r.q, r.q_o, m)
    save(r.w1, r.w1o, 0)
    gather.round()

    def make_v(i):
        m, rows = i // pere, pl.ds(pl.multiple_of(lax.rem(i, pere) * tile, tile), tile)
        r.v[m, rows] = (dot(r.normed[m, rows], matrix(1, 0)) + vector("b_value")).astype(BF16)

    loop(micro * pere, make_v)
    for m in range(micro):
        save(r.v, r.v_o, m)
    save(r.w1, r.w1o, 1)

    def turn_v(i):
        m, rows = i // (ext // WIN), pl.ds(pl.multiple_of(lax.rem(i, ext // WIN) * WIN, WIN), WIN)
        r.vT[m, :, rows] = r.v[m, rows].T

    loop(micro * (ext // WIN), turn_v)
    lane = lax.broadcasted_iota(jnp.int32, (WIN, WIN), 1)
    half0 = jnp.where(lane < HEAD, 1.0, 0.0).astype(BF16)
    half1 = jnp.where(lane < HEAD, 0.0, 1.0).astype(BF16)

    def attend_block(i, slot):
        m, b = i // count, lax.rem(i, count)
        rows = pl.ds(pl.multiple_of(b * WIN, WIN), WIN)
        keys = pl.ds(pl.multiple_of(b * WIN, WIN), 3 * WIN)
        left = r.band[0, jnp.where(b == 0, m, micro)]
        right = r.band[1, jnp.where(b == count - 1, m, micro)]

        def pair(n):
            lanes = pl.ds(n * 2 * HEAD, 2 * HEAD)
            k2 = r.k[m, keys, lanes]
            q2 = r.q[m, rows, lanes]
            both = jnp.concatenate([q2 * half0, q2 * half1], axis=0)
            s = dot_t(k2, both)
            parts = [
                s[:WIN] + jnp.concatenate([left, left], axis=1),
                s[WIN : 2 * WIN],
                s[2 * WIN :] + jnp.concatenate([right, right], axis=1),
            ]
            largest = functools.reduce(jnp.maximum, [jnp.max(p, axis=0, keepdims=True) for p in parts])
            powers = [jnp.exp(p - largest) for p in parts]
            total = sum(jnp.sum(p, axis=0, keepdims=True) for p in powers)
            scale = 1.0 / total
            p = jnp.concatenate([(e * scale).astype(BF16) for e in powers], axis=0)
            r.pstage[slot, n] = p
            out = dot(r.vT[m, lanes, keys], p).astype(BF16)
            r.mixT[m, pl.ds(n * 2 * HEAD, HEAD), rows] = out[:HEAD, :WIN]
            r.mixT[m, pl.ds(n * 2 * HEAD + HEAD, HEAD), rows] = out[HEAD:, WIN:]

        for n in range(HEADS // 2):
            pair(n)

    end_p = staged(micro * count, r.pstage, lambda i: r.pt_o.at[i], r.psem, attend_block, {3: gather.round})
    for m in range(micro):
        save(r.mixT, r.mixT_o, m)

    def after(m, slot):
        for h in range(per):
            rows = slice(h * tile, (h + 1) * tile)
            mixture = r.mixT[m, :, rows].T
            out = dot(mixture, matrix(1, 1)) + vector("b_output") + r.chars[m, rows].astype(F32)
            r.res[m, rows] = out
            low = normalize(out, vector("mid_gain"), vector("mid_shift")).astype(BF16)
            r.normed2[m, rows] = low
            r.stage[slot, :, rows] = low.T

    end()
    end = staged(micro, short, lambda m: r.normed2T_o.at[m], r.csem, after)
    for m in range(micro):
        save(r.res, r.res_o, m)
    gather.round()
    save(r.w1, r.w1o, 2)
    save(r.w1, r.w1o, 3)

    def rise(i, slot):
        j, m = i // micro, lax.rem(i, micro)

        def rise_rows(h):
            rows = pl.ds(pl.multiple_of(h * tile, tile), tile)
            w = r.w1[2 + j // 2, lax.rem(j, 2)].reshape(D, D)
            hidden = dot(r.normed2[m, rows], w) + r.vup[j, 0:1]
            active, slope = gelu_parts(hidden)
            active = active.astype(BF16)
            r.act[j, m, rows] = active
            r.gstage[slot, rows] = slope.astype(BF16)
            r.stage[slot, :, rows] = active.T

        loop(per, rise_rows)
        pltpu.make_async_copy(r.gstage.at[slot], r.gp_o.at[j, m], r.gsem.at[slot]).start()

    def gcopy(i):
        slot = lax.rem(i, 2)
        return pltpu.make_async_copy(r.gstage.at[slot], r.gp_o.at[i // micro, lax.rem(i, micro)], r.gsem.at[slot])

    def rise_after(i, slot):
        @pl.when(i >= 2)
        def _():
            gcopy(i - 2).wait()

        rise(i, slot)

    end()
    end = staged(
        4 * micro,
        short,
        lambda i: r.actT_o.at[i // micro, lax.rem(i, micro)],
        r.csem,
        rise_after,
        {2: gather.round, 5: gather.round},
    )
    half = nz // 2
    save(r.w2, r.w2o, 0)

    def fall(i):
        m, rows = i // per, pl.ds(pl.multiple_of(lax.rem(i, per) * tile, tile), tile)
        total = r.res[m, rows] + vector("b_down")
        for j in range(4):
            w = r.w2[0, j // 2, (j % 2) * half : (j % 2 + 1) * half].reshape(D, D)
            total = total + dot(r.act[j, m, rows], w)
        place_rows = pl.ds(pl.multiple_of(i * tile, tile), tile)
        for n in range(D // 128):
            r.res2[n, place_rows] = total[:, n * 128 : (n + 1) * 128]

    loop(micro * per, fall, {1: gather.round})
    groups = length // KER
    for k in range(KER):
        for m in range(micro):
            for n in range(D // 128):
                low = r.res2[n, pl.ds(m * length + k, groups, stride=KER)].astype(BF16)
                r.grp[k, m * groups : (m + 1) * groups, n * 128 : (n + 1) * 128] = low
    gather.round()
    total = jnp.broadcast_to(vector("b_conv"), (micro * groups, D))
    for k in range(KER):
        w = r.w2[1, k // 2, (k % 2) * half : (k % 2 + 1) * half].reshape(D, D)
        total = total + dot(r.grp[k], w)
    r.conv_o[...] = total
    curved, _ = gelu_parts(total)
    r.mol_o[...] = normalize(curved, vector("out_gain"), vector("out_shift")).astype(BF16)
    for k in range(KER):
        save(r.grp, r.grp_o, k)
    save(r.w2, r.w2o, 1)
    end()
    end_p()
    for i in range(4 * micro - 2, 4 * micro):
        gcopy(jnp.int32(i)).wait()
    for copy in copies:
        copy.wait()
    sender.finish()


def forward_call(nz, lens, bats, chars, mats, vec):
    micro, length, _ = chars.shape
    small = mats[0].shape[0]
    count, ext, groups = length // WIN, length + 2 * WIN, length // KER
    any_spec = pl.BlockSpec(memory_space=pl.ANY)
    vmem = pl.BlockSpec(memory_space=pltpu.VMEM)
    smem = pl.BlockSpec(memory_space=pltpu.SMEM)
    wd, wc = (w.reshape(2, 2 * small, D) for w in mats[5:])
    copies = gather_copies(nz) + 3
    w1 = (4, 2, 2, nz, 2, 2 * small, D)
    w2 = (2, 2, nz, 2, 2, 2, 2 * small, D)
    outs = dict(
        w1o=(w1, BF16),
        w2o=(w2, BF16),
        vfull=((16, D), F32),
        normedT_o=((micro, D, length), BF16),
        q_o=((micro, length, D), BF16),
        v_o=((micro, ext, D), BF16),
        kT_o=((micro, D, ext), BF16),
        pt_o=((micro * count, HEADS // 2, 3 * WIN, 2 * WIN), BF16),
        mixT_o=((micro, D, length), BF16),
        res_o=((micro, length, D), F32),
        normed2T_o=((micro, D, length), BF16),
        gp_o=((4, micro, length, D), BF16),
        actT_o=((4, micro, D, length), BF16),
        grp_o=((KER, micro * groups, D), BF16),
        conv_o=((micro * groups, D), F32),
        mol_o=((micro * groups, D), BF16),
    )
    in_vmem = ("vfull", "conv_o", "mol_o")
    scratch = dict(
        w1=pltpu.VMEM(w1, BF16),
        w2=pltpu.VMEM(w2, BF16),
        vecs=pltpu.VMEM((2, nz, 2, 2, 16, 128), BF16),
        own=pltpu.VMEM((2, 4, small, D), BF16),
        pre=pltpu.VMEM((2, 4, small, D), BF16),
        vup=pltpu.VMEM((4, 8, D), F32),
        hchars=pltpu.VMEM((micro, WIN, D), BF16),
        normed=pltpu.VMEM((micro, ext, D), BF16),
        q=pltpu.VMEM((micro, length, D), BF16),
        k=pltpu.VMEM((micro, ext, D), BF16),
        v=pltpu.VMEM((micro, ext, D), BF16),
        vT=pltpu.VMEM((micro, D, ext), BF16),
        stage=pltpu.VMEM((2, D, ext), BF16),
        pstage=pltpu.VMEM((2, HEADS // 2, 3 * WIN, 2 * WIN), BF16),
        mixT=pltpu.VMEM((micro, D, length), BF16),
        res=pltpu.VMEM((micro, length, D), F32),
        res2=pltpu.VMEM((D // 128, micro * length, 128), F32),
        normed2=pltpu.VMEM((micro, length, D), BF16),
        act=pltpu.VMEM((4, micro, length, D), BF16),
        gstage=pltpu.VMEM((2, length, D), BF16),
        grp=pltpu.VMEM((KER, micro * groups, D), BF16),
        band=pltpu.VMEM((2, micro + 1, WIN, WIN), F32),
        send_sems=pltpu.SemaphoreType.DMA((copies,)),
        recv_sems=pltpu.SemaphoreType.DMA((copies,)),
        csem=pltpu.SemaphoreType.DMA((2,)),
        psem=pltpu.SemaphoreType.DMA((2,)),
        wsem=pltpu.SemaphoreType.DMA((18,)),
        gsem=pltpu.SemaphoreType.DMA((2,)),
    )
    assert tuple(outs) + tuple(scratch) == ForwardRefs._fields[-len(outs) - len(scratch) :]
    done = pl.pallas_call(
        functools.partial(forward_kernel, nz, small),
        out_shape=tuple(jax.ShapeDtypeStruct(*o) for o in outs.values()),
        in_specs=[smem] * 2 + [vmem] * 9,
        out_specs=tuple(vmem if n in in_vmem else any_spec for n in outs),
        scratch_shapes=list(scratch.values()),
        compiler_params=pltpu.CompilerParams(
            collective_id=1, has_side_effects=True, vmem_limit_bytes=VMEM_LIMIT
        ),
        name="gather_forward",
    )(lens, bats, chars, *mats[:5], wd, wc, vec)
    return Saved(*done)


VMEM_LIMIT = 64 << 20


SCATTER_UNITS = (6, 7, 4, 5, 2, 3, 1, 0)
OWN_BLOCKS = 6
STAGES = 5


def scatter_shape(nz, part, phase):
    size = {"x": 2, "z": nz, "y": 2}
    columns, order = PARTS[part]
    axis = order[2 - phase]
    free = tuple(size[a] for a in ("x", "z", "y") if a in order[: 2 - phase])
    return (UNITS, size[axis] - 1) + free + (D // (4 * nz), columns.size)


class Scatter:
    def __init__(self, grid, sender, blocks, arrivals, staging, stage_sem, buffers, outs):
        self.grid, self.sender, self.blocks = grid, sender, blocks
        self.arrivals, self.staging, self.stage_sem = arrivals, staging, stage_sem
        self.out1, self.out2, self.fin = outs
        self.buffers = buffers
        self.core = grid.place.core
        self.entered = {}
        self.going = {}
        self.sent = {}
        self.last = []
        self.rounds = 0

    def slot(self, unit):
        return SCATTER_UNITS.index(unit) % OWN_BLOCKS

    def enter(self, unit, copies):
        self.entered[unit] = self.rounds
        self.going[unit] = copies

    def stage_copy(self, unit):
        n = SCATTER_UNITS.index(unit) % 2
        return pltpu.make_async_copy(self.arrivals.at[unit], self.staging.at[n], self.stage_sem.at[n])

    def arrival(self, part, phase):
        return self.buffers[3 * part + phase]

    def launch(self, unit, part, phase):
        columns, order = PARTS[part]
        axis, free = order[2 - phase], order[: 2 - phase]
        for n, (device, there) in enumerate(self.grid.peers(axis)):

            def src(there=there):
                index = self.grid.index(free, {axis: there()})
                return self.blocks.at[(self.slot(unit),) + index + (slice(None), columns)]

            def dst(n=n):
                return self.arrival(part, phase).at[unit, n]

            copy = self.sender.start(src, dst, device)
            self.going[unit, part].append(copy)
            self.sent.setdefault(unit, []).append(copy)

    def received(self, key):
        for copy in self.going.pop(key):
            copy().wait_recv()

    def add(self, unit, part, phase):
        columns, order = PARTS[part]
        free = [a for a in ("x", "z", "y") if a in order[: 2 - phase]]
        buffer = self.arrival(part, phase)
        count = 1
        for a in free:
            count *= self.grid.size[a]

        def some(i):
            given, rest = {}, i
            for a in reversed(free):
                given[a] = lax.rem(rest, self.grid.size[a])
                rest = rest // self.grid.size[a]
            index = (self.slot(unit),) + self.grid.index((), given) + (slice(None), columns)
            total = self.blocks[index].astype(F32)
            for n in range(buffer.shape[1]):
                total = total + buffer[(unit, n) + tuple(given[a] for a in free)].astype(F32)
            self.blocks[index] = total.astype(BF16)

        loop(count, some)

    def add_core(self, unit):
        n, slot = SCATTER_UNITS.index(unit) % 2, self.slot(unit)
        nz = self.grid.size["z"]

        def some(i):
            index = (i // (2 * nz), lax.rem(i // 2, nz), lax.rem(i, 2))
            total = self.blocks[(slot,) + index].astype(F32) + self.staging[(n,) + index].astype(F32)
            self.blocks[(slot,) + index] = total.astype(BF16)

        loop(4 * nz, some)

    def finish(self, unit):
        place = self.grid.place
        for part, (columns, _) in enumerate(PARTS):
            self.received((unit, part))
            total = self.blocks[self.slot(unit), place.x, place.z, place.y, :, columns].astype(F32)
            buffer = self.arrival(part, 2)
            for n in range(buffer.shape[1]):
                total = total + buffer[unit, n].astype(F32)
            if unit < 4:
                rows = total.shape[0] // 2
                self.fin[unit, 0, :, columns] = total[:rows]
                self.fin[unit, 1, :, columns] = total[rows:]
            else:
                self.out2[(unit - 4) // 2, unit % 2, :, columns] = total
        for copy in self.sent[unit]:
            copy().wait_send()
            self.sender.open.remove(copy)
        if unit < 4:
            self.out1[unit, self.core] = self.fin[unit, self.core]
            src = lambda: self.fin.at[unit, 1 - self.core]
            dst = lambda: self.out1.at[unit, self.core]
            self.last.append(self.sender.start(src, dst, place.partner))

    def round(self):
        r = self.rounds
        self.rounds += 1
        for unit in SCATTER_UNITS:
            stage = r - self.entered.get(unit, r + 1)
            if stage == 0:
                self.received(unit)
                self.stage_copy(unit).start()
            elif stage == 1:
                self.stage_copy(unit).wait()
                self.add_core(unit)
                for part in range(len(PARTS)):
                    self.going[unit, part] = []
                    self.launch(unit, part, 0)
            elif stage in (2, 3):
                for part in range(len(PARTS)):
                    self.received((unit, part))
                    self.going[unit, part] = []
                    self.add(unit, part, stage - 2)
                    self.launch(unit, part, stage - 1)
            elif stage == 4:
                self.finish(unit)

    def close(self):
        for copy in self.last:
            copy().wait_recv()


def scatter_copies(nz):
    return UNITS * len(PARTS) * (nz + 1) + 4 + 16 + 4 + (nz + 2) + 4


def norm_back(x, dy, gain):
    centered = x - jnp.mean(x, axis=-1, keepdims=True)
    scale = lax.rsqrt(jnp.mean(centered * centered, axis=-1, keepdims=True) + EPSILON)
    hat = centered * scale
    g = dy * gain
    dx = scale * (g - jnp.mean(g, axis=-1, keepdims=True) - hat * jnp.mean(g * hat, axis=-1, keepdims=True))
    return dx, dy * hat


class BackwardRefs(typing.NamedTuple):
    conv: typing.Any
    cot: typing.Any
    vfull: typing.Any
    grp: typing.Any
    w1: typing.Any
    w2: typing.Any
    nT_h: typing.Any
    q_h: typing.Any
    v_h: typing.Any
    kT_h: typing.Any
    pt_h: typing.Any
    mixT_h: typing.Any
    res_h: typing.Any
    n2T_h: typing.Any
    gp_h: typing.Any
    actT_h: typing.Any
    chars_h: typing.Any
    grad: typing.Any
    out1: typing.Any
    out2: typing.Any
    outv: typing.Any
    arrivals: typing.Any
    blocks: typing.Any
    staging: typing.Any
    fin: typing.Any
    dres: typing.Any
    low: typing.Any
    dh: typing.Any
    acc: typing.Any
    wbuf: typing.Any
    slots: typing.Any
    resb: typing.Any
    q: typing.Any
    pts: typing.Any
    nT: typing.Any
    dqT: typing.Any
    edge: typing.Any
    hsend: typing.Any
    hrecv: typing.Any
    vg: typing.Any
    vgu: typing.Any
    gv: typing.Any
    gvc: typing.Any
    gvy: typing.Any
    gvx: typing.Any
    gvz: typing.Any
    send_sems: typing.Any
    recv_sems: typing.Any
    stage_sem: typing.Any
    wsem: typing.Any
    lsem: typing.Any
    gsem: typing.Any
    rsem: typing.Any
    psem: typing.Any
    osem: typing.Any


def backward_kernel(nz, small, *refs):
    known = len(BackwardRefs._fields)
    r = BackwardRefs(*refs[:known])
    grid = Grid(nz)
    place = grid.place
    x, y, z, core = place.x, place.y, place.z, place.core
    sender = Sender(r.send_sems, r.recv_sems)
    micro, length = r.q.shape[0], r.q.shape[1]
    count, ext, groups = length // WIN, length + 2 * WIN, length // KER
    half = nz // 2
    scatter = Scatter(
        grid, sender, r.blocks, r.arrivals, r.staging, r.stage_sem, refs[known:], (r.out1, r.out2, r.fin)
    )

    def vector(name):
        n = VECTORS.index(name)
        return r.vfull[n : n + 1, :]

    def note(name, rows):
        n = VECTORS.index(name)
        r.vg[n : n + 1, :] += jnp.sum(rows, axis=0, keepdims=True)

    def fetch(n):
        def copy(src):
            return pltpu.make_async_copy(src, r.wbuf.at[lax.rem(n, 3)], r.wsem.at[lax.rem(n, 3)])

        ranges = ((0, 4, lambda i: r.w2.at[1, i]), (4, 8, lambda i: r.w2.at[0, i]), (8, 12, lambda i: r.w1.at[4 + i]))
        for low, high, src in ranges:

            @pl.when((n >= low) & (n < high))
            def _():
                copy(src(n - low)).start()

        @pl.when(n == 12)
        def _():
            copy(r.w1.at[3]).start()

        @pl.when(n > 12)
        def _():
            copy(r.w1.at[jnp.minimum(n, 15) - 13]).start()

    def fetched(n):
        pltpu.make_async_copy(r.w1.at[0], r.wbuf.at[lax.rem(n, 3)], r.wsem.at[lax.rem(n, 3)]).wait()

    first_load = pltpu.make_async_copy(r.grp, r.dh.at[:, 0, pl.ds(0, micro * groups)], r.psem.at[0])
    first_load.start()
    for n in range(2):
        fetch(jnp.int32(n))
    short = pl.ds(0, length)

    def act_copy(j):
        slot = lax.rem(j, 2)
        return pltpu.make_async_copy(r.actT_h.at[j], r.slots.at[slot, :, :, short], r.lsem.at[slot])

    for j in range(2):
        act_copy(jnp.int32(j)).start()

    def gp_copy(i):
        slot = lax.rem(i, 2)
        return pltpu.make_async_copy(r.gp_h.at[i // micro, lax.rem(i, micro)], r.q.at[slot], r.gsem.at[slot])

    for i in range(2):
        gp_copy(jnp.int32(i)).start()
    n_copy = pltpu.make_async_copy(r.nT_h, r.nT, r.osem.at[1])
    n_copy.start()
    r.vg[...] = jnp.zeros_like(r.vg)
    r.vgu[...] = jnp.zeros_like(r.vgu)
    greet(place)

    conv = r.conv[...]
    curved, slope = gelu_parts(conv)
    cot = r.cot[...].astype(F32)
    d_curved, gains = norm_back(curved, cot, vector("out_gain"))
    note("out_gain", gains)
    note("out_shift", cot)
    d_conv = d_curved * slope
    note("b_conv", d_conv)
    r.low[0, : micro * groups] = d_conv.astype(BF16)
    wide = D // 2
    first_load.wait()

    def conv_block(k):
        fetched(k)
        fetch(k + 2)
        low = r.low[0, : micro * groups]
        back = dot_t(low, r.wbuf[lax.rem(k, 3)])
        for n in range(D // 128):
            for m in range(micro):
                part = back[m * groups : (m + 1) * groups, n * 128 : (n + 1) * 128]
                r.dres[n, pl.ds(m * length + k, groups, stride=KER)] = part

    def split_block(k, product, unit):
        slot = OWN_BLOCKS + lax.rem(k, 2)

        def some(i):
            out = product(i).astype(BF16).reshape(2, 2, 2, 2 * small, D)
            for c in range(2):
                for h in range(2):
                    r.blocks[slot, c, h * half + i] = out[:, c, h]
            for h in range(2):
                mine = r.blocks[slot, core, h * half + i]
                r.blocks[scatter.slot(unit + h), k // 2, lax.rem(k, 2) * half + i] = mine

        loop(half, some)

    first_sends = {}

    def split_copies(unit):
        for h in range(2):
            first_sends[unit + h] = []
            for k in range(4):

                def src(h=h, k=k):
                    return r.blocks.at[OWN_BLOCKS + k % 2, 1 - core, pl.ds(h * half, half)]

                def dst(h=h, k=k):
                    return r.arrivals.at[unit + h, k // 2, pl.ds(k % 2 * half, half)]

                first_sends[unit + h].append(sender.hold(src, dst, place.partner))

    def send_split(k, unit):
        for h in range(2):
            first_sends[unit + h][k]().start()

    def split_wait(k, unit):
        for h in range(2):
            first_sends[unit + h][k]().wait_send()

    split_copies(6)
    split_copies(4)

    def conv_grad(k):
        def product(i):
            lanes = pl.ds(pl.multiple_of(i * wide, 128), wide)
            return dot(r.dh[k, 0, : micro * groups, lanes].T, r.low[0, : micro * groups])

        split_block(k, product, 6)

    def conv_step(k):
        conv_block(k)
        for n in range(2, 4):
            pl.when(k == n)(functools.partial(split_wait, n - 2, 6))
        conv_grad(k)

    loop(KER, conv_step, {k: functools.partial(send_split, k, 6) for k in range(KER)})
    for k in range(2, 4):
        split_wait(k, 6)
    scatter.enter(6, first_sends[6])
    scatter.enter(7, first_sends[7])

    def dres_rows(rows):
        return jnp.concatenate([r.dres[n, rows] for n in range(D // 128)], axis=1)

    tile = 256
    per = length // tile

    def lower(i):
        m, rows = i // per, pl.ds(pl.multiple_of(lax.rem(i, per) * tile, tile), tile)
        value = dres_rows(pl.ds(pl.multiple_of(i * tile, tile), tile))
        note("b_down", value)
        r.low[m, rows] = value.astype(BF16)

    loop(micro * per, lower)
    scatter.round()

    def down_step(j):
        n = 4 + j
        fetched(n)
        fetch(n + 2)

        def some(m):
            gp_copy(j * micro + m).wait()

            def part(h):
                rows = pl.ds(pl.multiple_of(h * tile, tile), tile)
                back = dot_t(r.low[m, rows], r.wbuf[lax.rem(n, 3)]).astype(BF16).astype(F32)
                back = back * r.q[lax.rem(j * micro + m, 2), rows].astype(F32)
                r.vgu[j, 0:1] += jnp.sum(back, axis=0, keepdims=True)
                r.dh[j, m, rows] = back.astype(BF16)

            loop(per, part)

            @pl.when(j * micro + m + 2 < 4 * micro)
            def _():
                gp_copy(j * micro + m + 2).start()

        loop(micro, some)
        act_copy(j).wait()
        for n in range(2, 4):
            pl.when(j == n)(functools.partial(split_wait, n - 2, 4))

        def product(i):
            rows = pl.ds(pl.multiple_of(i * wide, 128), wide)
            return sum(dot(r.slots[lax.rem(j, 2), m, rows, short], r.low[m]) for m in range(micro))

        split_block(j, product, 4)

        @pl.when(j < 2)
        def _():
            act_copy(j + 2).start()

    def down_hook(k):
        send_split(k, 4)
        if k in (0, 2):
            scatter.round()

    loop(4, down_step, {k: functools.partial(down_hook, k) for k in range(4)})
    q_copy = pltpu.make_async_copy(r.q_h, r.q, r.osem.at[0])
    q_copy.start()
    turned = [
        pltpu.make_async_copy(r.n2T_h, r.slots.at[0, :, :, short], r.lsem.at[0]),
        pltpu.make_async_copy(r.mixT_h, r.slots.at[1, :, :, short], r.lsem.at[1]),
    ]
    for copy in turned:
        copy.start()
    for k in range(2, 4):
        split_wait(k, 4)
    scatter.enter(4, first_sends[4])
    scatter.enter(5, first_sends[5])
    scatter.round()

    def res_copy(i):
        rows = pl.ds(pl.multiple_of(lax.rem(i, per) * tile, tile), tile)
        return pltpu.make_async_copy(r.res_h.at[i // per, rows], r.resb.at[lax.rem(i, 2)], r.rsem.at[lax.rem(i, 2)])

    for i in range(2):
        res_copy(jnp.int32(i)).start()

    def grad_block(slot, left, right):
        def some(i):
            rows = pl.ds(pl.multiple_of(i * wide, 128), wide)
            out = sum(dot(left(m, rows), right(m)) for m in range(micro))
            r.blocks[slot, i] = out.astype(BF16).reshape(nz, 2, 2 * small, D)

        loop(2, some)

    def send_block(unit, slot):
        return sender.start(lambda: r.blocks.at[slot], lambda: r.arrivals.at[unit], place.partner)

    turned[0].wait()
    sends = {}

    def up_grad(i):
        t, mine = i // 2, lax.rem(i, 2)
        j = 2 * t + jnp.where(mine == 1, core, 1 - core)
        slot = jnp.where(mine == 1, scatter.slot(2) + t, OWN_BLOCKS + t)
        grad_block(slot, lambda m, rows: r.slots[0, m, rows, short], lambda m: r.dh[j, m])

    def up_send(t):
        sends[2 + t] = send_block(2 + t, OWN_BLOCKS + t)

    loop(4, up_grad, {0: functools.partial(up_send, 0), 2: functools.partial(up_send, 1)})
    scatter.enter(2, [sends[2]])
    scatter.enter(3, [sends[3]])
    scatter.round()

    def up_back(j):
        n = 8 + j
        fetched(n)
        fetch(n + 2)

        def some(i):
            m, rows = i // per, pl.ds(pl.multiple_of(lax.rem(i, per) * tile, tile), tile)
            out = dot_t(r.dh[j, m, rows], r.wbuf[lax.rem(n, 3)])
            all_rows = pl.ds(pl.multiple_of(i * tile, tile), tile)

            @pl.when(j == 0)
            def _():
                r.acc[all_rows] = out

            @pl.when(j > 0)
            def _():
                r.acc[all_rows] += out

        loop(micro * per, some)

    loop(4, up_back, {1: scatter.round})

    def mid_norm(i):
        m, rows = i // per, pl.ds(pl.multiple_of(lax.rem(i, per) * tile, tile), tile)
        all_rows = pl.ds(pl.multiple_of(i * tile, tile), tile)
        res_copy(i).wait()
        dy = r.acc[all_rows]
        dx, gains = norm_back(r.resb[lax.rem(i, 2)], dy, vector("mid_gain"))

        @pl.when(i + 2 < micro * per)
        def _():
            res_copy(i + 2).start()

        note("mid_gain", gains)
        note("mid_shift", dy)
        total = dres_rows(all_rows) + dx
        note("b_output", total)
        for n in range(D // 128):
            r.dres[n, all_rows] = total[:, n * 128 : (n + 1) * 128]
        low = total.astype(BF16)
        r.low[m, rows] = low

    loop(micro * per, mid_norm)
    scatter.round()

    fetched(jnp.int32(12))
    fetch(jnp.int32(14))

    def mix_back(i):
        m, rows = i // per, pl.ds(pl.multiple_of(lax.rem(i, per) * tile, tile), tile)
        r.dh[3, m, rows] = dot_t(r.low[m, rows], r.wbuf[0]).astype(BF16)

    loop(micro * per, mix_back)
    for t in range(2):
        sends[2 + t]().wait_send()
        sender.open.remove(sends[2 + t])
    turned[1].wait()
    grad_block(
        jnp.where(core == 1, scatter.slot(1), OWN_BLOCKS),
        lambda m, rows: r.slots[1, m, rows, short],
        lambda m: r.low[m],
    )
    value_send = sender.hold(lambda: r.blocks.at[OWN_BLOCKS], lambda: r.arrivals.at[1], place.partner)
    pl.when(core == 0)(lambda: value_send().start())
    attn = [
        pltpu.make_async_copy(r.v_h, r.slots.at[0], r.lsem.at[0]),
        pltpu.make_async_copy(r.kT_h, r.slots.at[1], r.lsem.at[1]),
    ]
    for copy in attn:
        copy.start()

    lane = lax.broadcasted_iota(jnp.int32, (WIN, WIN), 1)
    half0 = jnp.where(lane < HEAD, 1.0, 0.0).astype(BF16)
    half1 = jnp.where(lane < HEAD, 0.0, 1.0).astype(BF16)
    blocks = micro * count

    turnaround = jnp.where(x == 0, count - 1, 0)

    def where(i):
        return lax.rem(i // count, micro), lax.rem(lax.rem(i, count) + turnaround, count)

    def pt_copy(i):
        m, b = where(i)
        return pltpu.make_async_copy(r.pt_h.at[m * count + b], r.pts.at[lax.rem(i, 2)], r.psem.at[lax.rem(i, 2)])

    def two_heads(ref, m, rows, lanes):
        both = ref[m, rows, lanes]
        return jnp.concatenate([both * half0, both * half1], axis=0)

    there = pl.multiple_of((1 - x) * (length + WIN), WIN)
    edge = pl.multiple_of((1 - x) * (length - WIN), WIN)

    def close_rows(which, m, target):
        def some(b):
            target[m, pl.ds(pl.multiple_of(b * WIN, WIN), WIN)] = r.acc[
                pl.ds(pl.multiple_of((b + 1) * WIN, WIN), WIN)
            ].astype(BF16)

        loop(count, some)
        r.edge[m] = r.acc[pl.ds(pl.multiple_of(edge + WIN, WIN), WIN)]

    halos = {}

    def halo_send(which, m):
        def src():
            return r.hsend.at[which, m]

        halos[which, m] = sender.start(src, lambda: r.hrecv.at[which, m], place.across_x)

    def halo_close(which, target):
        for m in range(micro):
            halos[which, m]().wait_recv()
            target[m, pl.ds(edge, WIN)] = (r.edge[m] + r.hrecv[which, m].astype(F32)).astype(BF16)

    def attention(start, pair, target, which, hooks):
        def step(i):
            m, b = where(i)

            @pl.when(lax.rem(i, count) == 0)
            def _():
                def clear(n):
                    r.acc[pl.ds(pl.multiple_of(n * WIN, WIN), WIN)] = jnp.zeros((WIN, D), F32)

                loop(ext // WIN, clear)

            pt_copy(start + i).wait()
            rows = pl.ds(pl.multiple_of(b * WIN, WIN), WIN)
            keys = pl.ds(pl.multiple_of(b * WIN, WIN), 3 * WIN)

            def one(n):
                pair(n, m, rows, keys, lax.rem(start + i, 2))

            for n in range(HEADS // 2):
                one(n)

            @pl.when(start + i + 2 < 2 * blocks)
            def _():
                pt_copy(start + i + 2).start()

            @pl.when(lax.rem(i, count) == 0)
            def _():
                r.hsend[which, m] = r.acc[pl.ds(there, WIN)].astype(BF16)

            @pl.when(lax.rem(i, count) == count - 1)
            def _():
                close_rows(which, m, target)

        merged = {count * m: [functools.partial(halo_send, which, m)] for m in range(micro)}
        for at, hook in hooks.items():
            merged.setdefault(at, []).append(hook)

        def run(several):
            for hook in several:
                hook()

        loop(blocks, step, {at: functools.partial(run, several) for at, several in merged.items()})

    def value_pair(n, m, rows, keys, slot):
        lanes = pl.ds(n * 2 * HEAD, 2 * HEAD)
        r.acc[keys, lanes] += dot(r.pts[slot, n], two_heads(r.dh.at[3], m, rows, lanes))

    for i in range(2):
        pt_copy(jnp.int32(i)).start()
    attention(0, value_pair, r.dh.at[2], 0, {})
    for copy in attn + [q_copy, n_copy]:
        copy.wait()
    scatter.round()

    def score_pair(n, m, rows, keys, slot):
        lanes = pl.ds(n * 2 * HEAD, 2 * HEAD)
        d_attend = dot_t(r.slots[0, m, keys, lanes], two_heads(r.dh.at[3], m, rows, lanes))
        p = r.pts[slot, n].astype(F32)
        weighted = p * d_attend
        inner = jnp.sum(weighted, axis=0, keepdims=True)
        d_scores = (weighted - p * inner).astype(BF16)
        r.acc[keys, lanes] += dot(d_scores, two_heads(r.q, m, rows, lanes))
        out = (dot(r.slots[1, m, lanes, keys], d_scores) * HEAD ** (-0.5)).astype(BF16)
        r.dqT[m, pl.ds(n * 2 * HEAD, HEAD), rows] = out[:HEAD, :WIN]
        r.dqT[m, pl.ds(n * 2 * HEAD + HEAD, HEAD), rows] = out[HEAD:, WIN:]

    def value_grad():
        halo_close(0, r.dh.at[2])
        grad_block(
            jnp.where(core == 0, scatter.slot(1), OWN_BLOCKS), lambda m, rows: r.nT[m, rows], lambda m: r.dh[2, m]
        )
        pl.when(core == 1)(lambda: value_send().start())

    attention(blocks, score_pair, r.dh.at[1], 1, {0: value_grad, 4: scatter.round})
    sender.open.append(value_send)
    scatter.enter(1, [value_send])
    chars_copy = pltpu.make_async_copy(r.chars_h, r.q, r.osem.at[0])
    chars_copy.start()

    fetch(jnp.int32(15))

    def turn(i):
        m, rows = i // per, pl.ds(pl.multiple_of(lax.rem(i, per) * tile, tile), tile)
        r.dh[0, m, rows] = r.dqT[m, :, rows].T

    loop(micro * per, turn)

    query_send = sender.hold(lambda: r.blocks.at[OWN_BLOCKS + 1], lambda: r.arrivals.at[0], place.partner)

    def query_grad(i):
        pl.when(i == 1)(functools.partial(halo_close, 1, r.dh.at[1]))
        slot = jnp.where(i == core, scatter.slot(0), OWN_BLOCKS + 1)
        grad_block(slot, lambda m, rows: r.nT[m, rows], lambda m: r.dh[i, m])
        pl.when(i != core)(lambda: query_send().start())

    loop(2, query_grad)
    sender.open.append(query_send)
    scatter.enter(0, [query_send])
    scatter.round()
    for n in range(13, 16):
        fetched(jnp.int32(n))
    chars_copy.wait()

    def out_copy(i):
        rows = pl.ds(pl.multiple_of(lax.rem(i, per) * tile, tile), tile)
        return pltpu.make_async_copy(r.resb.at[lax.rem(i, 2)], r.grad.at[i // per, rows], r.rsem.at[lax.rem(i, 2)])

    def first_norm(i):
        m, rows = i // per, pl.ds(pl.multiple_of(lax.rem(i, per) * tile, tile), tile)
        all_rows = pl.ds(pl.multiple_of(i * tile, tile), tile)
        dq, dv = r.dh[0, m, rows], r.dh[2, m, rows]
        note("b_query", dq.astype(F32))
        note("b_value", dv.astype(F32))
        dy = dot_t(dq, r.wbuf[1]) + dot_t(r.dh[1, m, rows], r.wbuf[2]) + dot_t(dv, r.wbuf[0])
        dx, gains = norm_back(r.q[m, rows].astype(F32), dy, vector("pre_gain"))
        note("pre_gain", gains)
        note("pre_shift", dy)

        @pl.when(i >= 2)
        def _():
            out_copy(i - 2).wait()

        r.resb[lax.rem(i, 2)] = dres_rows(all_rows) + dx
        out_copy(i).start()

    loop(micro * per, first_norm, {1: scatter.round})

    group = 384 // small
    lane = lax.broadcasted_iota(jnp.int32, (384, group * 128), 1)
    row = lax.broadcasted_iota(jnp.int32, (384, group * 128), 0)

    def pieces(values, fields, groups):
        lanes, rows = lane[:, : groups * 128], row[:, : groups * 128]
        field = lax.rem(lanes, 128)
        pick = jnp.where((rows == lanes // 128 * fields + field) & (field < fields), 1.0, 0.0).astype(BF16)
        results = []
        for value in values:
            high = value.astype(BF16)
            rest = (value - high.astype(F32)).astype(BF16)
            results.append(dot(high, pick) + dot(rest, pick))
        return results

    def device_index(d):
        return d // (4 * nz), (d // 4) % nz, (d // 2) % 2, d % 2

    for g, out in enumerate(pieces([r.vg[:, g * 384 : (g + 1) * 384] for g in range(2)], small, group)):
        for n in range(group):
            r.gv[device_index(g * group + n)] = out[:, n * 128 : (n + 1) * 128]
    lines = [r.vgu[g // 2, :, (g % 2) * 384 : (g % 2 + 1) * 384] for g in range(8)]
    group4 = group // 4
    for g, out in enumerate(pieces(lines, 4 * small, group4)):
        for n in range(group4):
            at = len(VECTORS)
            r.gv[device_index(g * group4 + n) + (slice(at, at + 1),)] = out[0:1, n * 128 : (n + 1) * 128]

    send = sender.start(lambda: r.gv.at[:, :, :, 1 - core], lambda: r.gvc, place.partner)
    scatter.round()
    send().wait_recv()
    r.gvc[...] = r.gvc[...] + r.gv[:, :, :, core]
    send = sender.start(lambda: r.gvc.at[:, :, 1 - y], lambda: r.gvy, place.across_y)
    scatter.round()
    send().wait_recv()
    r.gvy[...] = r.gvy[...] + r.gvc[:, :, y]
    send = sender.start(lambda: r.gvy.at[1 - x], lambda: r.gvx, place.across_x)
    scatter.round()
    send().wait_recv()
    r.gvx[...] = r.gvx[...] + r.gvy[x]
    last = []
    for n, (device, index) in enumerate(grid.peers("z")):
        last.append(
            sender.start(lambda index=index: r.gvx.at[index()], lambda n=n: r.gvz.at[n], device)
        )
    while any(scatter.rounds - e < STAGES for e in scatter.entered.values()):
        scatter.round()
    for copy in last:
        copy().wait_recv()
    total = r.gvx[z]
    for n in range(nz - 1):
        total = total + r.gvz[n]
    r.outv[...] = total
    for i in range(micro * per - 2, micro * per):
        out_copy(jnp.int32(i)).wait()
    scatter.close()
    sender.finish()


def backward_call(nz, f, chars, cot):
    micro, length, _ = chars.shape
    small = D // (8 * nz)
    count, ext, groups = length // WIN, length + 2 * WIN, length // KER
    any_spec = pl.BlockSpec(memory_space=pl.ANY)
    vmem = pl.BlockSpec(memory_space=pltpu.VMEM)
    rows2 = 2 * small
    copies = scatter_copies(nz)
    sems = pltpu.SemaphoreType.DMA
    block = (2, nz, 2, rows2, D)
    scratch = dict(
        blocks=pltpu.VMEM((OWN_BLOCKS + 2,) + block, BF16),
        staging=pltpu.VMEM((2,) + block, BF16),
        fin=pltpu.VMEM((4, 2, small, D), F32),
        dres=pltpu.VMEM((D // 128, micro * length, 128), F32),
        low=pltpu.VMEM((micro, length, D), BF16),
        dh=pltpu.VMEM((4, micro, length, D), BF16),
        acc=pltpu.VMEM((micro * length, D), F32),
        wbuf=pltpu.VMEM((3, D, D), BF16),
        slots=pltpu.VMEM((2, micro, D, ext), BF16),
        resb=pltpu.VMEM((2, 256, D), F32),
        q=pltpu.VMEM((micro, length, D), BF16),
        pts=pltpu.VMEM((2, HEADS // 2, 3 * WIN, 2 * WIN), BF16),
        nT=pltpu.VMEM((micro, D, length), BF16),
        dqT=pltpu.VMEM((micro, D, length), BF16),
        edge=pltpu.VMEM((micro, WIN, D), F32),
        hsend=pltpu.VMEM((2, micro, WIN, D), BF16),
        hrecv=pltpu.VMEM((2, micro, WIN, D), BF16),
        vg=pltpu.VMEM((16, D), F32),
        vgu=pltpu.VMEM((4, 8, D), F32),
        gv=pltpu.VMEM((2, nz, 2, 2, 16, 128), F32),
        gvc=pltpu.VMEM((2, nz, 2, 16, 128), F32),
        gvy=pltpu.VMEM((2, nz, 16, 128), F32),
        gvx=pltpu.VMEM((nz, 16, 128), F32),
        gvz=pltpu.VMEM((nz - 1, 16, 128), F32),
        send_sems=sems((copies,)),
        recv_sems=sems((copies,)),
        stage_sem=sems((2,)),
        wsem=sems((3,)),
        lsem=sems((2,)),
        gsem=sems((2,)),
        rsem=sems((2,)),
        psem=sems((2,)),
        osem=sems((2,)),
    )
    assert tuple(scratch) == BackwardRefs._fields[-len(scratch) :]
    buffers = [pltpu.VMEM(scatter_shape(nz, part, phase), BF16) for part in range(len(PARTS)) for phase in range(3)]
    outs = (
        jax.ShapeDtypeStruct((micro, length, D), F32),
        jax.ShapeDtypeStruct((4, 2, small, D), F32),
        jax.ShapeDtypeStruct((2, 2, rows2, D), F32),
        jax.ShapeDtypeStruct((16, 128), F32),
        jax.ShapeDtypeStruct((UNITS,) + block, BF16),
    )
    w1 = f.w1o.reshape(8, D, D)
    w2 = f.w2o.reshape(2, 4, D, D)
    args = [f.conv_o, cot.reshape(micro * groups, D), f.vfull, f.grp_o, w1, w2, f.normedT_o, f.q_o]
    args += [f.v_o, f.kT_o, f.pt_o, f.mixT_o, f.res_o, f.normed2T_o, f.gp_o, f.actT_o, chars]
    grad, out1, out2, outv, _ = pl.pallas_call(
        functools.partial(backward_kernel, nz, small),
        out_shape=outs,
        in_specs=[vmem] * 3 + [any_spec] * 14,
        out_specs=(any_spec, vmem, vmem, vmem, any_spec),
        scratch_shapes=list(scratch.values()) + buffers,
        compiler_params=pltpu.CompilerParams(
            collective_id=2, has_side_effects=True, vmem_limit_bytes=VMEM_LIMIT
        ),
        name="backward_scatter",
    )(*args)
    return grad, out1, out2, outv


def band_rows(rows_all, block_count):
    return jnp.stack([rows_all[b * WIN : b * WIN + 3 * WIN] for b in range(block_count)])


def band_back(band_grads, block_count):
    total = None
    for b in range(block_count):
        padded = jnp.pad(band_grads[b], ((b * WIN, (block_count - 1 - b) * WIN), (0, 0), (0, 0)))
        total = padded if total is None else total + padded
    return total


def shifted(value, axis, steps):
    count = lax.axis_size(axis)
    initial, last = (max(0, -steps), min(count, count - steps))
    return lax.ppermute(value, axis, [(source, source + steps) for source in range(initial, last)])


def with_halo(x, width, dim):
    length = x.shape[dim]
    last = lax.slice_in_dim(x, length - width, length, axis=dim)
    initial = lax.slice_in_dim(x, 0, width, axis=dim)
    return jnp.concatenate([shifted(last, "seq", 1), x, shifted(initial, "seq", -1)], axis=dim)


def layer(mats, vecs, chars, cot, allowed):
    w_query, w_key, w_value, w_output, w_up, w_down, w_conv = mats
    v = {name: value.astype(F32) for name, value in vecs.items()}
    micro, block_len, _ = chars.shape
    count = block_len // WIN
    rows = micro * block_len
    source = chars.astype(F32).reshape(rows, D)
    normed = normalize(source, v["pre_gain"], v["pre_shift"]).astype(BF16)
    queries = (forward_dot(normed, w_query) + v["b_query"]).astype(BF16)
    key_rows = forward_dot(normed, w_key).astype(BF16)
    value_rows = (forward_dot(normed, w_value) + v["b_value"]).astype(BF16)
    stacked = jnp.stack([key_rows, value_rows]).reshape(2, micro, block_len, D)
    stacked = with_halo(stacked, WIN, 2)
    heads = stacked.reshape(2, micro, block_len + 2 * WIN, HEADS, HEAD)
    query_heads = queries.reshape(micro * count, WIN, HEADS, HEAD)
    key_band = jnp.concatenate([band_rows(heads[0, m], count) for m in range(micro)])
    value_band = jnp.concatenate([band_rows(heads[1, m], count) for m in range(micro)])
    scores = jnp.einsum("bqhe,bkhe->bhqk", query_heads, key_band, preferred_element_type=F32) * HEAD ** (-0.5)
    allowed = allowed.reshape(micro * count, 1, WIN, 3 * WIN)
    scores = jnp.where(allowed, scores, -1e30)
    largest = jnp.max(scores, axis=-1, keepdims=True)
    powers = jnp.exp(scores - largest)
    norm_sum = jnp.sum(powers, axis=-1, keepdims=True)
    attend = powers / norm_sum
    attend_low = attend.astype(BF16)
    mixture = jnp.einsum("bhqk,bkhe->bqhe", attend_low, value_band, preferred_element_type=F32)
    mixture = mixture.reshape(rows, D).astype(BF16)
    residual = source + (forward_dot(mixture, w_output) + v["b_output"])
    normed2 = normalize(residual, v["mid_gain"], v["mid_shift"]).astype(BF16)
    hidden = forward_dot(normed2, w_up) + v["b_up"]
    active = jax.nn.gelu(hidden).astype(BF16)
    residual2 = residual + (forward_dot(active, w_down) + v["b_down"])
    grouped = residual2.astype(BF16).reshape(rows // KER, KER * D)
    conv_out = forward_dot(grouped, w_conv) + v["b_conv"]
    curved = jax.nn.gelu(conv_out)
    result = normalize(curved, v["out_gain"], v["out_shift"]).astype(BF16)

    g = {}
    _, pullback = jax.vjp(normalize, curved, v["out_gain"], v["out_shift"])
    d_curved, g["out_gain"], g["out_shift"] = pullback(cot.astype(F32).reshape(rows // KER, D))
    _, pullback = jax.vjp(jax.nn.gelu, conv_out)
    (d_conv,) = pullback(d_curved)
    g["b_conv"] = jnp.sum(d_conv, axis=0)
    d_conv_low = d_conv.astype(BF16)
    g["w_conv"] = weight_grad(grouped, d_conv_low)
    d_res2 = input_grad(d_conv_low, w_conv).reshape(rows, D)
    g["b_down"] = jnp.sum(d_res2, axis=0)
    d_res2_low = d_res2.astype(BF16)
    g["w_down"] = weight_grad(active, d_res2_low)
    d_active = input_grad(d_res2_low, w_down)
    _, pullback = jax.vjp(jax.nn.gelu, hidden)
    (d_hidden,) = pullback(d_active)
    g["b_up"] = jnp.sum(d_hidden, axis=0)
    d_hidden_low = d_hidden.astype(BF16)
    g["w_up"] = weight_grad(normed2, d_hidden_low)
    d_normed2 = input_grad(d_hidden_low, w_up)
    _, pullback = jax.vjp(normalize, residual, v["mid_gain"], v["mid_shift"])
    d_middle, g["mid_gain"], g["mid_shift"] = pullback(d_normed2)
    d_res = d_res2 + d_middle
    g["b_output"] = jnp.sum(d_res, axis=0)
    d_res_low = d_res.astype(BF16)
    g["w_output"] = weight_grad(mixture, d_res_low)
    d_mix = input_grad(d_res_low, w_output).astype(BF16).reshape(micro * count, WIN, HEADS, HEAD)
    d_attend = jnp.einsum("bqhe,bkhe->bhqk", d_mix, value_band, preferred_element_type=F32)
    inner = jnp.sum(attend * d_attend, axis=-1, keepdims=True)
    d_scores = (attend * (d_attend - inner)).astype(BF16)
    d_value_band = jnp.einsum("bhqk,bqhe->bkhe", attend_low, d_mix, preferred_element_type=F32)
    d_query = jnp.einsum("bhqk,bkhe->bqhe", d_scores, key_band, preferred_element_type=F32) * HEAD ** (-0.5)
    d_key_band = jnp.einsum("bhqk,bqhe->bkhe", d_scores, query_heads, preferred_element_type=F32) * HEAD ** (-0.5)

    def merged(band):
        parts = band.reshape(micro, count, 3 * WIN, HEADS, HEAD)
        return jnp.stack([band_back(parts[m], count) for m in range(micro)])

    stacked = jnp.stack([merged(d_key_band), merged(d_value_band)])
    stacked = stacked.reshape(2, micro, block_len + 2 * WIN, D)
    from_below = shifted(stacked[:, :, block_len + WIN :].astype(BF16), "seq", 1).astype(F32)
    from_above = shifted(stacked[:, :, :WIN].astype(BF16), "seq", -1).astype(F32)
    middle = stacked[:, :, WIN : WIN + block_len]
    middle = middle + jnp.pad(from_below, ((0, 0), (0, 0), (0, block_len - WIN), (0, 0)))
    middle = middle + jnp.pad(from_above, ((0, 0), (0, 0), (block_len - WIN, 0), (0, 0)))
    d_key_low = middle[0].astype(BF16).reshape(rows, D)
    d_value_low = middle[1].astype(BF16).reshape(rows, D)
    d_query_low = d_query.reshape(rows, D).astype(BF16)
    g["w_query"] = weight_grad(normed, d_query_low)
    g["b_query"] = jnp.sum(d_query_low.astype(F32), axis=0)
    g["w_key"] = weight_grad(normed, d_key_low)
    g["w_value"] = weight_grad(normed, d_value_low)
    g["b_value"] = jnp.sum(d_value_low.astype(F32), axis=0)
    d_normed = input_grad(d_query_low, w_query) + input_grad(d_key_low, w_key) + input_grad(d_value_low, w_value)
    _, pullback = jax.vjp(normalize, source, v["pre_gain"], v["pre_shift"])
    d_source, g["pre_gain"], g["pre_shift"] = pullback(d_normed)
    return result.reshape(micro, rows // KER // micro, D), (d_res + d_source).reshape(chars.shape), g


PARAMS = (
    "pre_gain",
    "pre_shift",
    "w_query",
    "b_query",
    "w_key",
    "w_value",
    "b_value",
    "w_output",
    "b_output",
    "mid_gain",
    "mid_shift",
    "w_up",
    "b_up",
    "w_down",
    "b_down",
    "w_conv",
    "b_conv",
    "out_gain",
    "out_shift",
)
MATRICES = tuple(n for n in PARAMS if n.startswith("w_"))
VECTORS = tuple(n for n in PARAMS if n not in MATRICES + ("b_up",))


def allowed_pairs(row_lengths, row_batch, micro, block_len):
    seq_count = lax.axis_size("seq")
    seq_place = lax.axis_index("seq")
    count = block_len // WIN
    buffer_len = block_len * seq_count
    places = seq_place * block_len + jnp.arange(block_len, dtype=jnp.int32)
    band_start = seq_place * block_len - WIN + WIN * jnp.arange(count, dtype=jnp.int32)
    key_places = band_start[:, None] + jnp.arange(3 * WIN, dtype=jnp.int32)[None, :]
    flat_keys = key_places.reshape(-1)
    outside = (flat_keys < 0) | (flat_keys >= buffer_len)
    query_blocks = places.reshape(count, WIN)
    near = jnp.abs(query_blocks[:, :, None] - key_places[:, None, :]) <= WIN
    result = []
    for step in range(micro):
        query_segs = segment_ids(row_lengths[0], row_batch[0], step, places).reshape(count, WIN)
        key_segs = segment_ids(row_lengths[0], row_batch[0], step, flat_keys)
        key_segs = jnp.where(outside, -2, key_segs).reshape(count, 3 * WIN)
        result.append(near & (query_segs[:, :, None] == key_segs[:, None, :]))
    return jnp.stack(result)


def per_device(characters, *rest):
    params = dict(zip(PARAMS, rest[: len(PARAMS)]))
    row_lengths, row_batch, cot_molecules = rest[len(PARAMS) :]
    seq, dp = lax.axis_size("seq"), lax.axis_size("dp")
    small = params["w_query"].shape[0]
    nz = dp // 4
    fast = seq == 2 and dp % 4 == 0 and nz > 1 and small % 8 == 0 and small <= 32
    if fast:
        vec = jnp.zeros((16, 128), BF16)
        vec = vec.at[: len(VECTORS), :small].set(jnp.stack([params[n] for n in VECTORS]))
        vec = vec.at[len(VECTORS), : 4 * small].set(params["b_up"])
        chars = characters[:, 0]
        f = forward_call(nz, row_lengths, row_batch, chars, [params[n] for n in MATRICES], vec)
        result = f.mol_o.reshape(cot_molecules[:, 0].shape)
        grad_chars, out1, out2, outv = backward_call(nz, f, chars, cot_molecules[:, 0])
    else:
        allowed = allowed_pairs(row_lengths, row_batch, characters.shape[0], characters.shape[2])
        full = {n: lax.all_gather(params[n], AXES, axis=0, tiled=True) for n in PARAMS}
        mats = tuple(full[n] for n in MATRICES)
        full_vecs = {n: full[n] for n in VECTORS + ("b_up",)}
        result, grad_chars, g = layer(mats, full_vecs, characters[:, 0], cot_molecules[:, 0], allowed)
    if fast:
        out1 = out1.reshape(8, small, D)
        out2 = out2.reshape(2, 4 * small, D)
        done = {n: out1[i] for i, n in enumerate(MATRICES[:4])}
        done["w_up"] = out1[4:].transpose(1, 0, 2).reshape(small, 4 * D)
        done["w_down"], done["w_conv"] = out2[0], out2[1]
        done.update({n: outv[i, :small] for i, n in enumerate(VECTORS)})
        done["b_up"] = outv[len(VECTORS), : 4 * small]
    else:
        done = {n: lax.psum_scatter(g[n], AXES, scatter_dimension=0, tiled=True) for n in PARAMS}
    return (result[:, None], grad_chars[:, None]) + tuple(done[n] for n in PARAMS)


def solution(mesh):
    both = P(AXES)
    rows = P(AXES, None)
    acts = P(None, "dp", "seq", None)
    param_specs = tuple(rows if n in MATRICES else both for n in PARAMS)
    in_specs = (acts,) + param_specs + (P("dp", None), P("dp", None), acts)
    out_specs = (acts, acts) + param_specs
    return jax.shard_map(per_device, mesh=mesh, in_specs=in_specs, out_specs=out_specs, check_vma=False)
```

time: 617 us -> 291 us (0.47)
  matrix products: 172 us -> 0 us
  other arithmetic: 97 us -> 0 us
  local copies, waits for them, and re-layouts: 103 us -> 15 us
  Pallas kernels: 220 us -> 273 us
  starting transfers between devices: 11.5 us -> 0 us
    dot_general x27 -> x0, matrix products: 172 us -> none  [the longest x7 42.5 us: input_grad(): lax.dot_general(left, weight, (((1,), (1,)), ((), ())), preferred_element...]
    pallas_call x2, Pallas kernels: 220 us -> 273 us  [the longest x1 155 us: backward_call(): pl.pallas_call(functools.partial(backward_kernel, nz, small), out_shape=o...]
    another operation x5 -> x0, other arithmetic: 24.5 us -> none
    slice x6 -> x0, local copies, waits for them, and re-layouts: 23.7 us -> none  [the longest x2 12.2 us: per_device(): w_up = w1[4:].transpose(1, 0, 2).reshape(D, 4 * D)]
    sub x3 -> x0, other arithmetic: 23.4 us -> none  [the longest x1 23.4 us: layer(): powers = jnp.exp(scores - largest)]
    unnamed x187 -> x4, local copies, waits for them, and re-layouts: 21.1 us -> 3.43 us
    add x11 -> x0, other arithmetic: 14.8 us -> none  [the longest x4 10.8 us: band_back(): total = padded if total is None else total + padded]
    convert_element_type x9 -> x0, other arithmetic: 14 us -> none  [the longest x1 13.3 us: layer(): d_scores = (attend * (d_attend - inner)).astype(BF16)]
  transfers between devices with their start and end apart: 4 -> 0, of which waited for: 2 -> 0; matrix products, arithmetic and copies ran while one was open for 9% -> 0% of each run, Pallas kernels for 0% -> 0%
where the time goes in v2:
time: 291 us; the launch traced here: 289 us
  Pallas kernels  273 us (94%)
  local copies, waits for them, and re-layouts  15 us (5%)
    pallas_call x1, Pallas kernels, backward_call(): pl.pallas_call(functools.partial(backward_kernel, nz, small), out_shape=o...  155 us
    pallas_call x1, Pallas kernels, forward_call(): pl.pallas_call(functools.partial(forward_kernel, nz, small), out_shape=tu...  118 us

profile of v2, /device:TPU:0, one launch (start us, length us, event | category | flops | bytes accessed | tf_op | source)
XLA Modules:
  0.0 289.0 jit_solution(3172004811487464329)
XLA Ops:
  0.7 1.5 stack.47
  2.2 0.6 scatter.6
  2.8 1.3 scatter.9.refs_10_
  4.0 117.9 %gather_forward.1 = (bf16[4,2,2,4,2,48,768]{6,5,4,3,2,1,0:T(8,128)(2,1)}, bf16[2,2,4,2,2,2,48,768]{7,6,5,4,3,2,1,0:T(8,128)(2,1)}, f32[16,768]{1,0:T(8,128)}, bf...) custom-call(s32[1,4]{1,0:T(1,128)} %refs_0_.1, ...), custom_call_target="tpu_custom_call" | custom-call | tf_op jit(solution)/shard_map/gather_forward/pallas_call | solution.py:726
  121.9 155.4 %backward_scatter.1 = (f32[2,512,768]{2,1,0:T(8,128)}, f32[4,2,24,768]{3,2,1,0:T(8,128)}, f32[2,2,48,768]{3,2,1,0:T(8,128)}, f32[16,128]{1,0:T(8,128)}, bf16[8,2,4,2,48,768]{5,4,3,2,1,0:T(8,128)(2,1)}) custom-call(f32[256,768]{1,0:T(8,128)} %get-tuple-element.66.refs_0_, bf16[256,768]{1,0:T(8,128)(2,1)} %bitcast.71, f32[16,768]{1,0:T(8,128)} %get-tuple-element.67.refs_2_, ...), custom_call_target="tpu_custom_call" | custom-call | tf_op jit(solution)/shard_map/backward_scatter/pallas_call | solution.py:1571
  277.4 0.0 copy-start
  277.4 1.3 slice_bitcast_fusion.8
  278.7 1.5 slice_bitcast_fusion.4
  280.2 1.0 slice.112
  281.2 0.7 copy.47
  282.0 1.7 slice_bitcast_fusion
  283.7 1.9 fusion
  285.6 1.8 copy.51
  287.3 0.0 copy-done
  287.3 1.7 copy.52
Async XLA Ops:
  277.4 10.0 %copy-start = (f32[2,512,768]{2,1,0:T(8,128)S(1)}, f32[2,512,768]{2,1,0:T(8,128)}, u32[]{:S(2)}) copy-start(f32[2,512,768]{2,1,0:T(8,128)} %get-tuple-element.81) | copy-start | bytes 9437188

commit v3 on v2

--- a/solution.py
+++ b/solution.py
@@ -175,6 +175,8 @@
 
     def launch(self, unit, part, phase):
         columns, order = PARTS[part]
+        if unit < 2 and order[0] == "y":
+            order = PARTS[3][1]
         done, axis = order[:phase], order[phase]
 
         def block():
@@ -564,7 +566,7 @@
         for n in range(HEADS // 2):
             pair(n)
 
-    end_p = staged(micro * count, r.pstage, lambda i: r.pt_o.at[i], r.psem, attend_block, {3: gather.round})
+    end_p = staged(micro * count, r.pstage, lambda i: r.pt_o.at[i], r.psem, attend_block, {1: gather.round, 5: gather.round})
     for m in range(micro):
         save(r.mixT, r.mixT_o, m)
 
@@ -620,7 +622,7 @@
         lambda i: r.actT_o.at[i // micro, lax.rem(i, micro)],
         r.csem,
         rise_after,
-        {2: gather.round, 5: gather.round},
+        {5: gather.round},
     )
     half = nz // 2
     save(r.w2, r.w2o, 0)
@@ -769,8 +771,8 @@
     def slot(self, unit):
         return SCATTER_UNITS.index(unit) % OWN_BLOCKS
 
-    def enter(self, unit, copies):
-        self.entered[unit] = self.rounds
+    def enter(self, unit, copies, later=0):
+        self.entered[unit] = self.rounds + later
         self.going[unit] = copies
 
     def stage_copy(self, unit):
@@ -858,25 +860,29 @@
     def round(self):
         r = self.rounds
         self.rounds += 1
-        for unit in SCATTER_UNITS:
-            stage = r - self.entered.get(unit, r + 1)
-            if stage == 0:
-                self.received(unit)
-                self.stage_copy(unit).start()
-            elif stage == 1:
-                self.stage_copy(unit).wait()
-                self.add_core(unit)
-                for part in range(len(PARTS)):
-                    self.going[unit, part] = []
-                    self.launch(unit, part, 0)
-            elif stage in (2, 3):
-                for part in range(len(PARTS)):
-                    self.received((unit, part))
-                    self.going[unit, part] = []
-                    self.add(unit, part, stage - 2)
-                    self.launch(unit, part, stage - 1)
-            elif stage == 4:
-                self.finish(unit)
+        stages = {unit: r - at for unit, at in self.entered.items()}
+        for now in (1, 3, 2, 0, 4):
+            for unit in SCATTER_UNITS:
+                if stages.get(unit) == now:
+                    self.advance(unit, now)
+
+    def advance(self, unit, stage):
+        if stage == 0:
+            self.received(unit)
+            self.stage_copy(unit).start()
+        elif stage == 1:
+            self.stage_copy(unit).wait()
+            self.add_core(unit)
+        elif stage < 4:
+            for part in range(len(PARTS)):
+                self.received((unit, part))
+                self.add(unit, part, stage - 2)
+        else:
+            self.finish(unit)
+        if 0 < stage < 4:
+            for part in range(len(PARTS)):
+                self.going[unit, part] = []
+                self.launch(unit, part, stage - 1)
 
     def close(self):
         for copy in self.last:
@@ -1102,7 +1108,8 @@
     for k in range(2, 4):
         split_wait(k, 6)
     scatter.enter(6, first_sends[6])
-    scatter.enter(7, first_sends[7])
+    scatter.enter(7, first_sends[7], 1)
+    scatter.round()
 
     def dres_rows(rows):
         return jnp.concatenate([r.dres[n, rows] for n in range(D // 128)], axis=1)
@@ -1157,7 +1164,7 @@
 
     def down_hook(k):
         send_split(k, 4)
-        if k in (0, 2):
+        if k == 1:
             scatter.round()
 
     loop(4, down_step, {k: functools.partial(down_hook, k) for k in range(4)})
@@ -1172,7 +1179,7 @@
     for k in range(2, 4):
         split_wait(k, 4)
     scatter.enter(4, first_sends[4])
-    scatter.enter(5, first_sends[5])
+    scatter.enter(5, first_sends[5], 1)
     scatter.round()
 
     def res_copy(i):
@@ -1206,9 +1213,9 @@
         sends[2 + t] = send_block(2 + t, OWN_BLOCKS + t)
 
     loop(4, up_grad, {0: functools.partial(up_send, 0), 2: functools.partial(up_send, 1)})
+    scatter.round()
     scatter.enter(2, [sends[2]])
-    scatter.enter(3, [sends[3]])
-    scatter.round()
+    scatter.enter(3, [sends[3]], 1)
 
     def up_back(j):
         n = 8 + j
@@ -1252,8 +1259,7 @@
         low = total.astype(BF16)
         r.low[m, rows] = low
 
-    loop(micro * per, mid_norm)
-    scatter.round()
+    loop(micro * per, mid_norm, {1: scatter.round})
 
     fetched(jnp.int32(12))
     fetch(jnp.int32(14))
@@ -1274,6 +1280,7 @@
     )
     value_send = sender.hold(lambda: r.blocks.at[OWN_BLOCKS], lambda: r.arrivals.at[1], place.partner)
     pl.when(core == 0)(lambda: value_send().start())
+    scatter.round()
     attn = [
         pltpu.make_async_copy(r.v_h, r.slots.at[0], r.lsem.at[0]),
         pltpu.make_async_copy(r.kT_h, r.slots.at[1], r.lsem.at[1]),
@@ -1365,7 +1372,7 @@
             for hook in several:
                 hook()
 
-        loop(blocks, step, {at: functools.partial(run, several) for at, several in merged.items()})
+        loop(blocks, step, {at: functools.partial(run, merged[at]) for at in sorted(merged)})
 
     def value_pair(n, m, rows, keys, slot):
         lanes = pl.ds(n * 2 * HEAD, 2 * HEAD)
@@ -1396,10 +1403,10 @@
             jnp.where(core == 0, scatter.slot(1), OWN_BLOCKS), lambda m, rows: r.nT[m, rows], lambda m: r.dh[2, m]
         )
         pl.when(core == 1)(lambda: value_send().start())
-
-    attention(blocks, score_pair, r.dh.at[1], 1, {0: value_grad, 4: scatter.round})
+        scatter.enter(1, [value_send])
+
+    attention(blocks, score_pair, r.dh.at[1], 1, {0: value_grad, 2: scatter.round, 5: scatter.round})
     sender.open.append(value_send)
-    scatter.enter(1, [value_send])
     chars_copy = pltpu.make_async_copy(r.chars_h, r.q, r.osem.at[0])
     chars_copy.start()
 
@@ -1702,6 +1709,40 @@
     return result.reshape(micro, rows // KER // micro, D), (d_res + d_source).reshape(chars.shape), g
 
 
+def finish_kernel(out1, out2, grad, molecules, *refs):
+    outs, sems = refs[:-1], refs[-1]
+    pairs = enumerate(((grad, outs[0]), (molecules, outs[1])))
+    copies = [pltpu.make_async_copy(src, dst, sems.at[i]) for i, (src, dst) in pairs]
+    for copy in copies:
+        copy.start()
+    rows = out1.shape[2]
+    for m in range(4):
+        outs[2 + m][...] = out1[m // 2, m % 2]
+        outs[6][:, m * D : (m + 1) * D] = out1[2 + m // 2, m % 2]
+    for p in range(2):
+        for half in range(2):
+            outs[7 + p][half * 2 * rows : (half + 1) * 2 * rows] = out2[p, half]
+    for copy in copies:
+        copy.wait()
+
+
+def finish_call(out1, out2, grad, molecules):
+    small = out1.shape[2]
+    shapes = [(small, D)] * 4 + [(small, 4 * D)] + [(4 * small, D)] * 2
+    vmem = pl.BlockSpec(memory_space=pltpu.VMEM)
+    any_spec = pl.BlockSpec(memory_space=pl.ANY)
+    first = [jax.ShapeDtypeStruct(a.shape, a.dtype) for a in (grad, molecules)]
+    return pl.pallas_call(
+        finish_kernel,
+        out_shape=first + [jax.ShapeDtypeStruct(shape, F32) for shape in shapes],
+        in_specs=[vmem] * 4,
+        out_specs=[any_spec] * 2 + [vmem] * 7,
+        scratch_shapes=[pltpu.SemaphoreType.DMA((2,))],
+        compiler_params=pltpu.CompilerParams(vmem_limit_bytes=VMEM_LIMIT),
+        name="finish",
+    )(out1, out2, grad, molecules)
+
+
 PARAMS = (
     "pre_gain",
     "pre_shift",
@@ -1770,11 +1811,8 @@
         full_vecs = {n: full[n] for n in VECTORS + ("b_up",)}
         result, grad_chars, g = layer(mats, full_vecs, characters[:, 0], cot_molecules[:, 0], allowed)
     if fast:
-        out1 = out1.reshape(8, small, D)
-        out2 = out2.reshape(2, 4 * small, D)
-        done = {n: out1[i] for i, n in enumerate(MATRICES[:4])}
-        done["w_up"] = out1[4:].transpose(1, 0, 2).reshape(small, 4 * D)
-        done["w_down"], done["w_conv"] = out2[0], out2[1]
+        grad_chars, result, *matrices = finish_call(out1, out2, grad_chars, result)
+        done = dict(zip(MATRICES, matrices))
         done.update({n: outv[i, :small] for i, n in enumerate(VECTORS)})
         done["b_up"] = outv[len(VECTORS), : 4 * small]
     else:

time: 291 us -> 266 us (0.914)
  Pallas kernels: 273 us -> 259 us
  local copies, waits for them, and re-layouts: 15 us -> 6.11 us
    pallas_call x1, Pallas kernels: 155 us -> 138 us  [backward_call(): pl.pallas_call(functools.partial(backward_kernel, nz, small), out_shape=o...]
    pallas_call x0 -> x1, Pallas kernels: none -> 5.11 us  [finish_call(): pl.pallas_call(finish_kernel, out_shape=first + [jax.ShapeDtypeStruct(sha...]
    unnamed x4 -> x0, local copies, waits for them, and re-layouts: 3.43 us -> none
where the time goes in v3:
time: 266 us
  Pallas kernels  259 us (97%)
  local copies, waits for them, and re-layouts  6.11 us (2%)
    pallas_call x1, Pallas kernels, backward_call(): pl.pallas_call(functools.partial(backward_kernel, nz, small), out_shape=o...  138 us
    pallas_call x1, Pallas kernels, forward_call(): pl.pallas_call(functools.partial(forward_kernel, nz, small), out_shape=tu...  115 us

profile of v3, /device:TPU:0, one launch (start us, length us, event | category | flops | bytes accessed | tf_op | source)
XLA Modules:
  0.0 265.5 jit_solution(1474302639972458435)
XLA Ops:
  0.7 1.5 stack.47
  2.2 0.6 scatter.6
  2.8 1.3 scatter.9.refs_10_
  4.0 115.5 %gather_forward.1 = (bf16[4,2,2,4,2,48,768]{6,5,4,3,2,1,0:T(8,128)(2,1)}, bf16[2,2,4,2,2,2,48,768]{7,6,5,4,3,2,1,0:T(8,128)(2,1)}, f32[16,768]{1,0:T(8,128)}, bf...) custom-call(s32[1,4]{1,0:T(1,128)} %refs_0_.1, ...), custom_call_target="tpu_custom_call" | custom-call | tf_op jit(solution)/shard_map/gather_forward/pallas_call | solution.py:728
  119.5 138.0 %backward_scatter.1 = (f32[2,512,768]{2,1,0:T(8,128)}, f32[4,2,24,768]{3,2,1,0:T(8,128)}, f32[2,2,48,768]{3,2,1,0:T(8,128)}, f32[16,128]{1,0:T(8,128)}, bf16[8,2,4,2,48,768]{5,4,3,2,1,0:T(8,128)(2,1)}) custom-call(f32[256,768]{1,0:T(8,128)} %get-tuple-element.74.refs_0_, bf16[256,768]{1,0:T(8,128)(2,1)} %bitcast.53, f32[16,768]{1,0:T(8,128)} %get-tuple-element.75.refs_2_, ...), custom_call_target="tpu_custom_call" | custom-call | tf_op jit(solution)/shard_map/backward_scatter/pallas_call | solution.py:1578
  257.5 5.1 %finish.1 = (f32[2,512,768]{2,1,0:T(8,128)}, bf16[2,128,768]{2,1,0:T(8,128)(2,1)}, f32[24,768]{1,0:T(8,128)}, f32[24,768]{1,0:T(8,128)}, f32[24,768]{1,0:T(8,128...) custom-call(f32[4,2,24,768]{3,2,1,0:T(8,128)} %get-tuple-element.89.out1, ...), custom_call_target="tpu_custom_call" | custom-call | tf_op jit(solution)/shard_map/finish/pallas_call | solution.py:1735
  262.6 1.2 slice_bitcast_fusion.4
  263.8 1.5 slice_bitcast_fusion

commit v4 on v3

--- a/solution.py
+++ b/solution.py
@@ -747,12 +747,21 @@
 STAGES = 5
 
 
+SCATTER_PARTS = PARTS + ((PARTS[2][0], PARTS[3][1]),)
+
+
+def scatter_part(unit, part):
+    if part != 2:
+        return part, unit
+    return (4, unit) if unit < 4 else (2, unit - 4)
+
+
 def scatter_shape(nz, part, phase):
     size = {"x": 2, "z": nz, "y": 2}
-    columns, order = PARTS[part]
+    columns, order = SCATTER_PARTS[part]
     axis = order[2 - phase]
     free = tuple(size[a] for a in ("x", "z", "y") if a in order[: 2 - phase])
-    return (UNITS, size[axis] - 1) + free + (D // (4 * nz), columns.size)
+    return (4 if part in (2, 4) else UNITS, size[axis] - 1) + free + (D // (4 * nz), columns.size)
 
 
 class Scatter:
@@ -779,11 +788,12 @@
         n = SCATTER_UNITS.index(unit) % 2
         return pltpu.make_async_copy(self.arrivals.at[unit], self.staging.at[n], self.stage_sem.at[n])
 
-    def arrival(self, part, phase):
-        return self.buffers[3 * part + phase]
+    def arrival(self, unit, part, phase):
+        kind, at = scatter_part(unit, part)
+        return self.buffers[3 * kind + phase], at
 
     def launch(self, unit, part, phase):
-        columns, order = PARTS[part]
+        columns, order = SCATTER_PARTS[scatter_part(unit, part)[0]]
         axis, free = order[2 - phase], order[: 2 - phase]
         for n, (device, there) in enumerate(self.grid.peers(axis)):
 
@@ -792,7 +802,8 @@
                 return self.blocks.at[(self.slot(unit),) + index + (slice(None), columns)]
 
             def dst(n=n):
-                return self.arrival(part, phase).at[unit, n]
+                buffer, at = self.arrival(unit, part, phase)
+                return buffer.at[at, n]
 
             copy = self.sender.start(src, dst, device)
             self.going[unit, part].append(copy)
@@ -803,9 +814,9 @@
             copy().wait_recv()
 
     def add(self, unit, part, phase):
-        columns, order = PARTS[part]
+        columns, order = SCATTER_PARTS[scatter_part(unit, part)[0]]
         free = [a for a in ("x", "z", "y") if a in order[: 2 - phase]]
-        buffer = self.arrival(part, phase)
+        buffer, at = self.arrival(unit, part, phase)
         count = 1
         for a in free:
             count *= self.grid.size[a]
@@ -818,7 +829,7 @@
             index = (self.slot(unit),) + self.grid.index((), given) + (slice(None), columns)
             total = self.blocks[index].astype(F32)
             for n in range(buffer.shape[1]):
-                total = total + buffer[(unit, n) + tuple(given[a] for a in free)].astype(F32)
+                total = total + buffer[(at, n) + tuple(given[a] for a in free)].astype(F32)
             self.blocks[index] = total.astype(BF16)
 
         loop(count, some)
@@ -839,9 +850,9 @@
         for part, (columns, _) in enumerate(PARTS):
             self.received((unit, part))
             total = self.blocks[self.slot(unit), place.x, place.z, place.y, :, columns].astype(F32)
-            buffer = self.arrival(part, 2)
+            buffer, at = self.arrival(unit, part, 2)
             for n in range(buffer.shape[1]):
-                total = total + buffer[unit, n].astype(F32)
+                total = total + buffer[at, n].astype(F32)
             if unit < 4:
                 rows = total.shape[0] // 2
                 self.fin[unit, 0, :, columns] = total[:rows]
@@ -1563,7 +1574,7 @@
         osem=sems((2,)),
     )
     assert tuple(scratch) == BackwardRefs._fields[-len(scratch) :]
-    buffers = [pltpu.VMEM(scatter_shape(nz, part, phase), BF16) for part in range(len(PARTS)) for phase in range(3)]
+    buffers = [pltpu.VMEM(scatter_shape(nz, part, phase), BF16) for part in range(len(SCATTER_PARTS)) for phase in range(3)]
     outs = (
         jax.ShapeDtypeStruct((micro, length, D), F32),
         jax.ShapeDtypeStruct((4, 2, small, D), F32),

time: 266 us -> 268 us (level)
  no operation moved by 1% of the time
where the time goes in v4:
time: 268 us; the launch traced here: 267 us
  Pallas kernels  260 us (97%)
  local copies, waits for them, and re-layouts  6.11 us (2%)
    pallas_call x1, Pallas kernels, backward_call(): pl.pallas_call(functools.partial(backward_kernel, nz, small), out_shape=o...  140 us
    pallas_call x1, Pallas kernels, forward_call(): pl.pallas_call(functools.partial(forward_kernel, nz, small), out_shape=tu...  115 us

profile of v4, /device:TPU:0, one launch (start us, length us, event | category | flops | bytes accessed | tf_op | source)
XLA Modules:
  0.0 267.3 jit_solution(2496418536563252498)
XLA Ops:
  0.7 1.5 stack.47
  2.2 0.6 scatter.6
  2.8 1.3 scatter.9.refs_10_
  4.0 115.5 %gather_forward.1 = (bf16[4,2,2,4,2,48,768]{6,5,4,3,2,1,0:T(8,128)(2,1)}, bf16[2,2,4,2,2,2,48,768]{7,6,5,4,3,2,1,0:T(8,128)(2,1)}, f32[16,768]{1,0:T(8,128)}, bf...) custom-call(s32[1,4]{1,0:T(1,128)} %refs_0_.1, ...), custom_call_target="tpu_custom_call" | custom-call | tf_op jit(solution)/shard_map/gather_forward/pallas_call | solution.py:728
  119.5 139.8 %backward_scatter.1 = (f32[2,512,768]{2,1,0:T(8,128)}, f32[4,2,24,768]{3,2,1,0:T(8,128)}, f32[2,2,48,768]{3,2,1,0:T(8,128)}, f32[16,128]{1,0:T(8,128)}, bf16[8,2,4,2,48,768]{5,4,3,2,1,0:T(8,128)(2,1)}) custom-call(f32[256,768]{1,0:T(8,128)} %get-tuple-element.74.refs_0_, bf16[256,768]{1,0:T(8,128)(2,1)} %bitcast.53, f32[16,768]{1,0:T(8,128)} %get-tuple-element.75.refs_2_, ...), custom_call_target="tpu_custom_call" | custom-call | tf_op jit(solution)/shard_map/backward_scatter/pallas_call | solution.py:1589
  259.3 5.1 %finish.1 = (f32[2,512,768]{2,1,0:T(8,128)}, bf16[2,128,768]{2,1,0:T(8,128)(2,1)}, f32[24,768]{1,0:T(8,128)}, f32[24,768]{1,0:T(8,128)}, f32[24,768]{1,0:T(8,128...) custom-call(f32[4,2,24,768]{3,2,1,0:T(8,128)} %get-tuple-element.89.out1, ...), custom_call_target="tpu_custom_call" | custom-call | tf_op jit(solution)/shard_map/finish/pallas_call | solution.py:1746
  264.4 1.2 slice_bitcast_fusion.4
  265.6 1.5 slice_bitcast_fusion

commit v5 on v3

--- a/solution.py
+++ b/solution.py
@@ -1797,9 +1797,9 @@
     nz = dp // 4
     fast = seq == 2 and dp % 4 == 0 and nz > 1 and small % 8 == 0 and small <= 32
     if fast:
-        vec = jnp.zeros((16, 128), BF16)
-        vec = vec.at[: len(VECTORS), :small].set(jnp.stack([params[n] for n in VECTORS]))
-        vec = vec.at[len(VECTORS), : 4 * small].set(params["b_up"])
+        vec = jnp.pad(jnp.stack([params[n] for n in VECTORS]), ((0, 16 - len(VECTORS)), (0, 128 - small)))
+        wide = jnp.pad(params["b_up"], (0, 128 - 4 * small))
+        vec = jnp.where(lax.broadcasted_iota(jnp.int32, (16, 128), 0) == len(VECTORS), wide[None], vec)
         chars = characters[:, 0]
         f = forward_call(nz, row_lengths, row_batch, chars, [params[n] for n in MATRICES], vec)
         result = f.mol_o.reshape(cot_molecules[:, 0].shape)

time: 266 us -> 266 us (level)
  no operation moved by 1% of the time
where the time goes in v5:
time: 266 us
  Pallas kernels  260 us (98%)
  local copies, waits for them, and re-layouts  4.89 us (2%)
    pallas_call x1, Pallas kernels, backward_call(): pl.pallas_call(functools.partial(backward_kernel, nz, small), out_shape=o...  139 us
    pallas_call x1, Pallas kernels, forward_call(): pl.pallas_call(functools.partial(forward_kernel, nz, small), out_shape=tu...  115 us

profile of v5, /device:TPU:0, one launch (start us, length us, event | category | flops | bytes accessed | tf_op | source)
XLA Modules:
  0.0 266.0 jit_solution(5923747527976439679)
XLA Ops:
  0.7 0.7 pad.8
  1.3 1.5 stack.47
  2.8 0.7 pad_select_fusion.refs_10_
  3.5 115.3 %gather_forward.1 = (bf16[4,2,2,4,2,48,768]{6,5,4,3,2,1,0:T(8,128)(2,1)}, bf16[2,2,4,2,2,2,48,768]{7,6,5,4,3,2,1,0:T(8,128)(2,1)}, f32[16,768]{1,0:T(8,128)}, bf...) custom-call(s32[1,4]{1,0:T(1,128)} %refs_0_.1, ...), custom_call_target="tpu_custom_call" | custom-call | tf_op jit(solution)/shard_map/gather_forward/pallas_call | solution.py:728
  118.8 139.2 %backward_scatter.1 = (f32[2,512,768]{2,1,0:T(8,128)}, f32[4,2,24,768]{3,2,1,0:T(8,128)}, f32[2,2,48,768]{3,2,1,0:T(8,128)}, f32[16,128]{1,0:T(8,128)}, bf16[8,2,4,2,48,768]{5,4,3,2,1,0:T(8,128)(2,1)}) custom-call(f32[256,768]{1,0:T(8,128)} %get-tuple-element.50.refs_0_, bf16[256,768]{1,0:T(8,128)(2,1)} %bitcast.52, f32[16,768]{1,0:T(8,128)} %get-tuple-element.51.refs_2_, ...), custom_call_target="tpu_custom_call" | custom-call | tf_op jit(solution)/shard_map/backward_scatter/pallas_call | solution.py:1578
  258.0 5.1 %finish.1 = (f32[2,512,768]{2,1,0:T(8,128)}, bf16[2,128,768]{2,1,0:T(8,128)(2,1)}, f32[24,768]{1,0:T(8,128)}, f32[24,768]{1,0:T(8,128)}, f32[24,768]{1,0:T(8,128...) custom-call(f32[4,2,24,768]{3,2,1,0:T(8,128)} %get-tuple-element.65.out1, ...), custom_call_target="tpu_custom_call" | custom-call | tf_op jit(solution)/shard_map/finish/pallas_call | solution.py:1735
  263.1 1.2 slice_bitcast_fusion.4
  264.3 1.5 slice_bitcast_fusion
  (1 shorter events, 0.0 us)
